TPU v7x, 256 devices: a whole 4x4x8 slice. The times are simulated.
256 devices in a mesh: pool: 32 (over z_lo, y, core), tensor: 8 (over x, z_hi).
Axes of the slice: x: 4, y: 4, z: 8 (z_hi: 2, z_lo: 4; z = z_hi * 4 + z_lo), core: 2. Of those that a mesh axis runs over, the one named last changes fastest.
Arguments:
- queries: bfloat16 [512, 8192], P('pool', 'tensor'), may hold values from -6 to 6
- cache_keys: bfloat16 [512, 256, 1024], P('pool', None, 'tensor'), may hold values from -6 to 6
- cache_values: bfloat16 [512, 256, 1024], P('pool', None, 'tensor'), may hold values from -6 to 6
- context_lens: int32 [512], P('pool'), may hold values from 2 to 256
- prompt_keys: bfloat16 [1024, 32, 1024], P('pool', None, 'tensor'), may hold values from -6 to 6
- prompt_values: bfloat16 [1024, 32, 1024], P('pool', None, 'tensor'), may hold values from -6 to 6
- prompt_lens: int32 [1024], P('pool'), may hold values from 1 to 32
- matching: int32 [1024, 1], P('pool'), may hold values from 0 to 31; in each aligned block of 32 rows (0 to 31, 32 to 63, ...) at most 2 rows name the same one
- dest_seq: int32 [1024], P('pool'), may hold values from 0 to 15
- out_weight: bfloat16 [8192, 4096], P('tensor'), may hold values from -0.5 to 0.5
Outputs:
- projected: bfloat16 [512, 4096], P('pool', 'tensor')
Inputs may be any that keep to these rules, and one draw needn't show every extreme that they name: `matching`: among the 32 prompts of one group at most 2 name the same receiving group, and in some group exactly 2 do.
All inputs are finite; a program needn't handle non-finite values.
Results may differ from a plain program's by a relative error of at most 0.017.
Values may be sent and summed in bfloat16 or wider, within the bound.
No kernel may reach another device: no remote copies, remote signals or barrier semaphores. Data moves between devices by JAX's collectives and lax.ppermute only.
A program may use at most 128 MiB of HBM per device.

v0:
```python
import math

import jax
import jax.numpy as jnp
from jax import lax
from jax.sharding import PartitionSpec as P

HD = 128
CAP = 2


def slot_ranks(owners):
    row_count = owners.shape[-1]
    same_owner = owners[..., :, None] == owners[..., None, :]
    earlier = jnp.arange(row_count)[None, :] < jnp.arange(row_count)[:, None]
    return jnp.sum(jnp.where(same_owner & earlier, 1, 0), axis=-1).astype(jnp.int32)


def shards(
    queries,
    cache_keys,
    cache_values,
    context_lens,
    prompt_keys,
    prompt_values,
    prompt_lens,
    matching,
    dest_seq,
    out_weight,
):
    seq_dev, q_width = queries.shape
    cache_len = cache_keys.shape[1]
    kv_width = cache_keys.shape[2]
    groups = kv_width // HD
    repeat = q_width // kv_width
    pool_size = lax.axis_size("pool")
    prompt_dev = prompt_keys.shape[0]
    prompt_len = prompt_keys.shape[1]
    owners = matching[:, 0]
    all_keys, all_values, all_lens, all_owners, all_dests = (
        lax.all_gather(prompt_keys, "pool", axis=0, tiled=True),
        lax.all_gather(prompt_values, "pool", axis=0, tiled=True),
        lax.all_gather(prompt_lens, "pool", axis=0, tiled=True),
        lax.all_gather(owners, "pool", axis=0, tiled=True),
        lax.all_gather(dest_seq, "pool", axis=0, tiled=True),
    )
    own_group = lax.axis_index("pool")
    block_owners = all_owners.reshape(pool_size, prompt_dev)
    order_rank = slot_ranks(block_owners)
    slot_iota = jnp.arange(CAP)
    chosen = (
        (block_owners[:, None, :] == own_group)
        & (order_rank[:, None, :] == slot_iota[None, :, None])
    ).astype(jnp.int32)
    picker = chosen.astype(jnp.bfloat16)
    block_keys = all_keys.reshape(pool_size, prompt_dev, prompt_len, kv_width)
    block_values = all_values.reshape(pool_size, prompt_dev, prompt_len, kv_width)
    got_keys = (
        jnp.einsum("scp,sptd->sctd", picker, block_keys, preferred_element_type=jnp.float32)
        .astype(jnp.bfloat16)
        .reshape(pool_size * CAP, prompt_len, kv_width)
    )
    got_values = (
        jnp.einsum("scp,sptd->sctd", picker, block_values, preferred_element_type=jnp.float32)
        .astype(jnp.bfloat16)
        .reshape(pool_size * CAP, prompt_len, kv_width)
    )
    got_lens = (
        jnp.sum(chosen * all_lens.reshape(pool_size, 1, prompt_dev), axis=2)
        .astype(jnp.int32)
        .reshape(pool_size * CAP)
    )
    got_dests = (
        jnp.sum(chosen * all_dests.reshape(pool_size, 1, prompt_dev), axis=2)
        .astype(jnp.int32)
        .reshape(pool_size * CAP)
    )
    score_scale = 1.0 / math.sqrt(HD)
    query_heads = queries.reshape(seq_dev, groups, repeat, HD)
    cache_k = cache_keys.reshape(seq_dev, cache_len, groups, HD)
    cache_v = cache_values.reshape(seq_dev, cache_len, groups, HD)
    cache_scores = (
        jnp.einsum("sgrd,scgd->sgrc", query_heads, cache_k, preferred_element_type=jnp.float32)
        * score_scale
    )
    cache_alive = jnp.arange(cache_len)[None, :] < context_lens[:, None]
    cache_scores = jnp.where(cache_alive[:, None, None, :], cache_scores, -jnp.inf)
    slot_count = got_keys.shape[0]
    slot_onehot = got_dests[:, None] == jnp.arange(seq_dev)[None, :]
    slot_pick = slot_onehot.astype(jnp.bfloat16)
    slot_table = slot_onehot.astype(jnp.float32)
    slot_q = jnp.einsum(
        "ks,sgrd->kgrd", slot_pick, query_heads, preferred_element_type=jnp.float32
    ).astype(jnp.bfloat16)
    recv_k = got_keys.reshape(slot_count, prompt_len, groups, HD)
    recv_v = got_values.reshape(slot_count, prompt_len, groups, HD)
    recv_scores = (
        jnp.einsum("kgrd,ktgd->kgrt", slot_q, recv_k, preferred_element_type=jnp.float32)
        * score_scale
    )
    recv_alive = jnp.arange(prompt_len)[None, :] < got_lens[:, None]
    recv_scores = jnp.where(recv_alive[:, None, None, :], recv_scores, -jnp.inf)
    slot_top = jnp.max(recv_scores, axis=-1)
    joined_top = jnp.max(
        jnp.where(slot_onehot.T[:, :, None, None], slot_top[None], -jnp.inf), axis=1
    )
    row_top = jnp.maximum(jnp.max(cache_scores, axis=-1), joined_top)
    slot_row_top = jnp.einsum("ks,sgr->kgr", slot_table, row_top, precision=lax.Precision.HIGHEST)
    cache_exp = jnp.exp(cache_scores - row_top[..., None])
    recv_exp = jnp.exp(recv_scores - slot_row_top[..., None])
    slot_den = jnp.sum(recv_exp, axis=-1)
    denominator = jnp.sum(cache_exp, axis=-1) + jnp.einsum(
        "ks,kgr->sgr", slot_table, slot_den, precision=lax.Precision.HIGHEST
    )
    weighted = jnp.einsum(
        "sgrc,scgd->sgrd",
        cache_exp.astype(jnp.bfloat16),
        cache_v,
        preferred_element_type=jnp.float32,
    )
    slot_weighted = jnp.einsum(
        "kgrt,ktgd->kgrd", recv_exp.astype(jnp.bfloat16), recv_v, preferred_element_type=jnp.float32
    )
    weighted = weighted + jnp.einsum(
        "ks,kgrd->sgrd", slot_table, slot_weighted, precision=lax.Precision.HIGHEST
    )
    attended = (weighted / denominator[..., None]).astype(jnp.bfloat16).reshape(seq_dev, q_width)
    partial_value = jnp.dot(attended, out_weight, preferred_element_type=jnp.float32)
    return lax.psum_scatter(
        partial_value.astype(jnp.bfloat16), "tensor", scatter_dimension=1, tiled=True
    )


def solution(mesh):
    placed = (
        P("pool", "tensor"),
        P("pool", None, "tensor"),
        P("pool", None, "tensor"),
        P("pool"),
        P("pool", None, "tensor"),
        P("pool", None, "tensor"),
        P("pool"),
        P("pool", None),
        P("pool"),
        P("tensor", None),
    )
    return jax.shard_map(
        shards, mesh=mesh, in_specs=placed, out_specs=P("pool", "tensor"), check_vma=False
    )
```

profile of v0, /device:TPU:6, one launch (start us, length us, event | category | flops | bytes accessed | tf_op | source)
XLA Modules:
  0.0 266.6 jit_solution(11917094232691834607)
XLA Ops:
  6.5 0.0 copy-start
  6.5 0.0 all-gather.4.cloned.1.call-start
  6.5 0.7 all-gather.4.cloned.1.call-update
  7.3 0.0 all-gather.6.cloned.1.call-start
  7.3 0.7 all-gather.6.cloned.1.call-update
  8.0 0.0 reduce-scatter.2.cloned.1.call-start
  8.1 1.3 dynamic-slice
  10.0 0.9 dynamic-update-slice.1
  10.9 0.8 dynamic-update-slice.2
  11.7 0.7 bitcast_dynamic-update-slice_fusion
  12.4 142.0 %all-reduce.3 = (s32[1024]{0:T(1024)S(1)}, s32[1024]{0:T(1024)S(1)}, s32[1024]{0:T(1024)S(1)}) all-reduce(s32[1024]{0:T(1024)S(1)} %bitcast_dynamic-update-slice_fusion, s32[1024]{0:T(1024)S(1)} %dynamic-update-slice.2, s32[1024]{0:T(1024)S(1)} %dynamic-update-slice.1), channel_id=2, replica_groups=mesh['pool'=32,'tensor'=8] {'pool'}, use_global_device_ids=true, to_apply=%add | all-reduce | flops 3072 | bytes 24576
  154.4 0.1 broadcast_in_dim_reshape.2
  154.5 0.1 mul.36
  154.5 0.1 mul.39
  154.6 0.8 select_reduce_fusion
  155.4 1.2 select_reduce_fusion.2
  156.6 0.1 eq.71
  156.7 0.1 lt.60
  156.8 0.8 copy.58
  157.6 0.7 iota_compare_fusion.2
  158.3 0.1 iota_compare_fusion
  158.4 1.0 convolution_convert_fusion.1
  159.4 0.0 copy-done
  159.4 0.5 fusion.41
  159.8 0.0 all-gather.4.cloned.1.call-done
  159.9 6.0 %fusion.4 = bf16[32,2,32,128]{3,1,2,0:T(2,128)(2,1)S(1)} fusion(bf16[32,32,32,128]{3,2,1,0:T(8,128)(2,1)} %bitcast.39, pred[32,32]{1,0:T(8,128)(4,1)S(1)} %broadcast_compare_fusion, s32[32,32]{1,0:T(8,128)S(1)} %select_reduce_fusion), kind=kOutput, calls=%fused_computation.5 | convolution fusion | flops 17047552 | bytes 8918016 | tf_op jit(solution)/shard_map/scp,sptd->sctd/dot_general | solution.py:59
  165.9 0.0 copy-start.1
  165.9 0.1 copy.45
  166.0 0.5 fusion.42
  166.5 0.1 copy.47
  166.5 0.1 select_reduce_fusion.1
  166.7 0.2 fusion.22
  166.8 0.1 copy.53
  166.9 0.2 fusion.31
  167.1 0.2 fusion.16
  167.4 0.2 convolution_add_fusion.1
  167.5 0.1 copy.54
  167.6 0.0 all-gather.6.cloned.1.call-done
  167.6 6.0 %fusion.7 = bf16[32,2,32,128]{3,1,2,0:T(2,128)(2,1)S(1)} fusion(bf16[32,32,32,128]{3,2,1,0:T(8,128)(2,1)} %bitcast.38, pred[32,32]{1,0:T(8,128)(4,1)S(1)} %broadcast_compare_fusion, s32[32,32]{1,0:T(8,128)S(1)} %select_reduce_fusion), kind=kOutput, calls=%fused_computation.6 | convolution fusion | flops 17047552 | bytes 8918016 | tf_op jit(solution)/shard_map/scp,sptd->sctd/dot_general | solution.py:64
  173.6 0.1 copy.50
  173.8 0.3 fusion.18
  174.1 0.2 fusion.14
  174.3 0.0 copy-done.1
  174.3 0.3 fusion.13
  174.6 5.2 %convolution_convert_fusion = bf16[16,4096]{1,0:T(8,128)(2,1)} fusion(bf16[1024,4096]{1,0:T(8,128)(2,1)} %param.19, bf16[2,8,8,128]{3,2,1,0:T(8,128)(2,1)S(1)} %bitcast.42), kind=kOutput, calls=%fused_computation.4 | convolution fusion | flops 134283264 | bytes 8552448 | tf_op jit(solution)/shard_map/dot_general | solution.py:128
  179.9 0.0 reduce-scatter.2.cloned.1.call-update
  179.9 80.1 %reduce-scatter.2.cloned.1.call-done = bf16[16,512]{1,0:T(8,128)(2,1)} async-done(((bf16[16,4096]{1,0:T(8,128)(2,1)}), bf16[16,512]{1,0:T(8,128)(2,1)}) %reduce-scatter.2.cloned.1.call-update) | async-done | bytes 16400 | tf_op jit(solution)/shard_map/reduce_scatter | solution.py:129
  (7 shorter events, 0.0 us)
Async XLA Ops:
  6.5 152.9 %copy-start = (bf16[16,256,128]{2,1,0:T(8,128)(2,1)S(1)}, bf16[16,256,128]{2,1,0:T(8,128)(2,1)}, u32[]{:S(2)}) copy-start(bf16[16,256,128]{2,1,0:T(8,128)(2,1)} %param.11) | copy-start | bytes 3145732
  6.5 153.3 %all-gather.4.cloned.1.call-start = ((), (), s32[]{:S(2)}) async-start(), calls=%async_computation.1 | async-start | bytes 8650752 | tf_op jit(solution)/shard_map/all_gather | solution.py:41
  7.3 160.4 %all-gather.6.cloned.1.call-start = ((), (), s32[]{:S(2)}) async-start(), calls=%async_computation.2 | async-start | bytes 8650752 | tf_op jit(solution)/shard_map/all_gather | solution.py:42
  8.0 252.0 %reduce-scatter.2.cloned.1.call-start = ((), (), s32[]{:S(2)}) async-start(), calls=%async_computation.3 | async-start | bytes 147456 | tf_op jit(solution)/shard_map/reduce_scatter | solution.py:129
  165.9 8.4 %copy-start.1 = (bf16[16,256,128]{2,1,0:T(8,128)(2,1)S(1)}, bf16[16,256,128]{2,1,0:T(8,128)(2,1)}, u32[]{:S(2)}) copy-start(bf16[16,256,128]{2,1,0:T(8,128)(2,1)} %param.12) | copy-start | bytes 3145732
Sparse Core Ops, SparseCore 0:
  9.2 72.4 all-gather.3
  83.5 68.1 all-gather.5
  180.0 79.9 reduce-scatter.1
where the time goes:
time: 267 us
  blocking collectives  142 us (53%)
  waiting for transfers between devices  81.6 us (31%)
  matrix products  20.5 us (8%)
  between operations  13.9 us (5%)
  local copies, waits for them, and re-layouts  5.31 us (2%)
  other arithmetic  3.27 us (1%)
    unnamed x1, blocking collectives  142 us
    reduce_scatter x1, waiting for transfers between devices, shards(): lax.psum_scatter(partial_value.astype(jnp.bfloat16), 'tensor', scatter_di...  80.1 us
    dot_general x1, matrix products, shards(): jnp.einsum('scp,sptd->sctd', picker, block_values, preferred_element_type...  6.03 us
    dot_general x1, matrix products, shards(): jnp.einsum('scp,sptd->sctd', picker, block_keys, preferred_element_type=j...  6.02 us
  transfers between devices with their start and end apart: 3, of which 1 were waited for; matrix products, arithmetic and copies ran while one was open for 6% of the time, Pallas kernels for 0%

commit v1 on v0

v1 whole, which is shorter than its diff:
```python
import functools
import math

import jax
import jax.numpy as jnp
from jax import lax
from jax.experimental import pallas as pl
from jax.experimental.pallas import tpu as pltpu
from jax.sharding import PartitionSpec as P

HD = 128
CAP = 2
NEG = -(2.0**99)
VMEM = pltpu.VMEM
SMEM = pltpu.SMEM
NT = (((1,), (1,)), ((), ()))


def pack_kernel(half, owner_ref, dest_ref, len_ref, keys_ref, values_ref, out_ref, count, index, length, target):
    prompts, plen, _ = keys_ref.shape
    blocks = out_ref.shape[0]
    width = CAP * plen
    my_half = lax.axis_index("pool") // half
    for i in range(2 * half):
        count[i] = 0
    for i in range(blocks * 2 * CAP):
        index[i] = 0
        length[i] = 0
        target[i] = 0
    for p in range(prompts):
        group = owner_ref[p, 0]
        rank = count[group]
        count[group] = rank + 1
        other = jnp.where(group // half == my_half, 0, 1)
        slot = (group % half) * (2 * CAP) + other * CAP + jnp.minimum(rank, CAP - 1)
        index[slot] = p
        length[slot] = len_ref[p]
        target[slot] = dest_ref[p]
    row = lax.broadcasted_iota(jnp.int32, (16, 128), 0)
    lane = lax.broadcasted_iota(jnp.int32, (16, 128), 1)
    pos = lane % plen
    second = (lane // plen) % CAP == 1
    lower = row < 8
    for b in range(blocks):
        for other in range(2):
            for r in range(CAP):
                p = index[b * 2 * CAP + other * CAP + r]
                at = other * 2 * width + r * plen
                out_ref[b, at : at + plen, :] = keys_ref[p]
                out_ref[b, at + width : at + width + plen, :] = values_ref[p]
        s = b * 2 * CAP
        limit = jnp.where(
            lower,
            jnp.where(second, length[s + 1], length[s]),
            jnp.where(second, length[s + 3], length[s + 2]),
        )
        code = jnp.where(
            lower,
            jnp.where(second, target[s + 1], target[s]),
            jnp.where(second, target[s + 3], target[s + 2]),
        )
        code = jnp.where(pos < limit, code, -1)
        out_ref[b, 4 * width :, :] = code.astype(jnp.float32).astype(jnp.bfloat16)


def split_heads(q_ref, scratch):
    seqs = q_ref.shape[0]
    heads = q_ref.shape[1] // HD
    for h in range(heads):
        scratch[h * seqs : (h + 1) * seqs, :] = q_ref[:, h * HD : (h + 1) * HD].astype(jnp.float32)
    return [scratch[pl.ds(s, heads, stride=seqs), :] for s in range(seqs)]


def prompt_scores(q, got_ref, other, scale):
    blocks, rows, _ = got_ref.shape
    width = (rows - 16) // 4
    at = other * 2 * width
    seq = lax.broadcasted_iota(jnp.int32, (q.shape[0], 128), 0) // 8
    left = lax.broadcasted_iota(jnp.int32, (8, 128), 1) < width
    out = []
    for b in range(0, blocks, 2):
        keys = jnp.concatenate([got_ref[b, at : at + width, :], got_ref[b + 1, at : at + width, :]], axis=0)
        s = lax.dot_general(q, keys, NT, preferred_element_type=jnp.float32) * scale
        meta0 = got_ref[b, 4 * width :, :].astype(jnp.float32)
        meta1 = got_ref[b + 1, 4 * width :, :].astype(jnp.float32)
        code = jnp.where(left, meta0[other * 8 : other * 8 + 8], meta1[other * 8 : other * 8 + 8])[0:1]
        out.append(jnp.where(seq == code.astype(jnp.int32), s, NEG))
    return out


def prompt_sum(weights, got_ref, other):
    blocks, rows, _ = got_ref.shape
    width = (rows - 16) // 4
    at = other * 2 * width + width
    total = None
    for i, b in enumerate(range(0, blocks, 2)):
        values = jnp.concatenate([got_ref[b, at : at + width, :], got_ref[b + 1, at : at + width, :]], axis=0)
        part = jnp.dot(weights[i].astype(jnp.bfloat16), values, preferred_element_type=jnp.float32)
        total = part if total is None else total + part
    return total


def partner_kernel(scale, q_ref, got_ref, out_ref, scratch):
    q = jnp.concatenate(split_heads(q_ref, scratch), axis=0).astype(jnp.bfloat16)
    scores = prompt_scores(q, got_ref, 1, scale)
    top = functools.reduce(jnp.maximum, scores)
    top = jnp.max(top, axis=1, keepdims=True).astype(jnp.bfloat16).astype(jnp.float32)
    exps = [jnp.exp(s - top) for s in scores]
    total = jnp.sum(functools.reduce(jnp.add, exps), axis=1, keepdims=True)
    rows = q.shape[0]
    out_ref[:rows, :] = prompt_sum(exps, got_ref, 1).astype(jnp.bfloat16)
    high = total.astype(jnp.bfloat16).astype(jnp.float32)
    lane = lax.broadcasted_iota(jnp.int32, (rows, 128), 1)
    stats = jnp.where(lane == 0, top, jnp.where(lane == 1, high, total - high))
    out_ref[rows:, :] = jnp.transpose(stats)[:16, :].astype(jnp.bfloat16)


def main_kernel(scale, lens_ref, q_ref, keys_ref, values_ref, got_ref, out_ref, top_ref, sum_ref, scratch):
    seqs, ctx, _ = keys_ref.shape
    rows = split_heads(q_ref, scratch)
    q = jnp.concatenate(rows, axis=0).astype(jnp.bfloat16)
    heads = q.shape[0] // seqs
    col = lax.broadcasted_iota(jnp.int32, (heads, ctx), 1)
    cache = []
    for s in range(seqs):
        sc = lax.dot_general(rows[s].astype(jnp.bfloat16), keys_ref[s], NT, preferred_element_type=jnp.float32)
        cache.append(jnp.where(col < lens_ref[s], sc * scale, NEG))
    scores = prompt_scores(q, got_ref, 0, scale)
    cache_all = jnp.concatenate(cache, axis=0)
    top = functools.reduce(jnp.maximum, scores + [cache_all[:, i : i + 128] for i in range(0, ctx, 128)])
    top = jnp.max(top, axis=1, keepdims=True)
    cache_exp = jnp.exp(cache_all - top)
    exps = [jnp.exp(s - top) for s in scores]
    total = functools.reduce(jnp.add, exps + [cache_exp[:, i : i + 128] for i in range(0, ctx, 128)])
    total = jnp.sum(total, axis=1, keepdims=True)
    parts = []
    for s in range(seqs):
        w = cache_exp[s * heads : (s + 1) * heads].astype(jnp.bfloat16)
        parts.append(jnp.dot(w, values_ref[s], preferred_element_type=jnp.float32))
    out_ref[...] = jnp.concatenate(parts, axis=0) + prompt_sum(exps, got_ref, 0)
    top_ref[...] = jnp.broadcast_to(top, top_ref.shape)
    sum_ref[...] = jnp.broadcast_to(total, sum_ref.shape)


def project_kernel(main_ref, top_ref, sum_ref, back_ref, weight_ref, out_ref, scratch):
    pieces, seqs, cols = out_ref.shape
    rows = main_ref.shape[0]
    heads = rows // seqs
    stats = jnp.concatenate([back_ref[rows:, :].astype(jnp.float32)] * (128 // 16), axis=0)
    stats = jnp.transpose(stats)
    far_top = stats[:, 0:1]
    far_sum = stats[:, 1:2] + stats[:, 2:3]
    top = jnp.maximum(top_ref[...], far_top)
    near = jnp.exp(top_ref[...] - top)
    far = jnp.exp(far_top - top)
    total = sum_ref[...] * near + far_sum * far
    scratch[...] = (main_ref[...] * near + back_ref[:rows, :].astype(jnp.float32) * far) / total
    attended = jnp.concatenate(
        [scratch[pl.ds(h, seqs, stride=heads), :].astype(jnp.bfloat16) for h in range(heads)], axis=1
    )
    for c in range(pieces):
        part = jnp.dot(attended, weight_ref[:, c * cols : (c + 1) * cols], preferred_element_type=jnp.float32)
        out_ref[c] = part.astype(out_ref.dtype)


def vmem(n):
    return [pl.BlockSpec(memory_space=VMEM)] * n


def smem(n):
    return [pl.BlockSpec(memory_space=SMEM)] * n


def shards(
    queries,
    cache_keys,
    cache_values,
    context_lens,
    prompt_keys,
    prompt_values,
    prompt_lens,
    matching,
    dest_seq,
    out_weight,
):
    seqs, q_width = queries.shape
    ctx = cache_keys.shape[1]
    prompts, plen, _ = prompt_keys.shape
    pool = lax.axis_size("pool")
    pieces = lax.axis_size("tensor")
    out_cols = out_weight.shape[1]
    half = pool // 2
    rows = q_width // HD * seqs
    width = CAP * plen
    scale = 1.0 / math.sqrt(HD)
    swap = [(i, (i + half) % pool) for i in range(pool)]
    halves = [list(range(half)), list(range(half, pool))]
    far_queries = lax.ppermute(queries, "pool", swap)
    packed = pl.pallas_call(
        functools.partial(pack_kernel, half),
        out_shape=jax.ShapeDtypeStruct((half, 4 * width + 16, HD), jnp.bfloat16),
        in_specs=smem(3) + vmem(2),
        out_specs=pl.BlockSpec(memory_space=VMEM),
        scratch_shapes=[
            SMEM((pool,), jnp.int32),
            SMEM((half * 2 * CAP,), jnp.int32),
            SMEM((half * 2 * CAP,), jnp.int32),
            SMEM((half * 2 * CAP,), jnp.int32),
        ],
        name="pack",
    )(matching, dest_seq, prompt_lens, prompt_keys, prompt_values)
    got = lax.all_to_all(packed, "pool", 0, 0, axis_index_groups=halves)
    back = pl.pallas_call(
        functools.partial(partner_kernel, scale),
        out_shape=jax.ShapeDtypeStruct((rows + 16, HD), jnp.bfloat16),
        in_specs=vmem(2),
        out_specs=pl.BlockSpec(memory_space=VMEM),
        scratch_shapes=[VMEM((rows, HD), jnp.float32)],
        compiler_params=pltpu.CompilerParams(vmem_limit_bytes=16 << 20),
        name="partner",
    )(far_queries, got)
    back = lax.ppermute(back, "pool", swap)
    main, top, total = pl.pallas_call(
        functools.partial(main_kernel, scale),
        out_shape=[jax.ShapeDtypeStruct((rows, HD), jnp.float32)] * 3,
        in_specs=smem(1) + vmem(4),
        out_specs=vmem(3),
        scratch_shapes=[VMEM((rows, HD), jnp.float32)],
        compiler_params=pltpu.CompilerParams(vmem_limit_bytes=24 << 20),
        cost_estimate=pl.CostEstimate(flops=200_000_000, bytes_accessed=4_000_000, transcendentals=200_000),
        name="main",
    )(context_lens, queries, cache_keys, cache_values, got)
    parts = pl.pallas_call(
        project_kernel,
        out_shape=jax.ShapeDtypeStruct((pieces, seqs, out_cols // pieces), jnp.bfloat16),
        in_specs=vmem(5),
        out_specs=pl.BlockSpec(memory_space=VMEM),
        scratch_shapes=[VMEM((rows, HD), jnp.float32)],
        compiler_params=pltpu.CompilerParams(vmem_limit_bytes=24 << 20),
        name="project",
    )(main, top, total, back, out_weight)
    parts = lax.all_to_all(parts, "tensor", 0, 0)
    return jnp.sum(parts.astype(jnp.float32), axis=0).astype(jnp.bfloat16)


def solution(mesh):
    placed = (
        P("pool", "tensor"),
        P("pool", None, "tensor"),
        P("pool", None, "tensor"),
        P("pool"),
        P("pool", None, "tensor"),
        P("pool", None, "tensor"),
        P("pool"),
        P("pool", None),
        P("pool"),
        P("tensor", None),
    )
    return jax.shard_map(
        shards, mesh=mesh, in_specs=placed, out_specs=P("pool", "tensor"), check_vma=False
    )
```

time: 267 us -> 58.8 us (0.22)
  blocking collectives: 142 us -> 18.6 us
  waiting for transfers between devices: 81.6 us -> 14.9 us
  matrix products: 20.5 us -> 0 us
  between operations: 13.9 us -> 0.06 us
  starting transfers between devices: 0.08 us -> 12.5 us
  Pallas kernels: 0 us -> 6.42 us
    unnamed x1 -> x0, blocking collectives: 142 us -> none
    reduce_scatter x1 -> x0, waiting for transfers between devices: 80.1 us -> none  [shards(): lax.psum_scatter(partial_value.astype(jnp.bfloat16), 'tensor', scatter_di...]
    dot_general x11 -> x0, matrix products: 20.5 us -> none  [the longest x1 6.03 us: shards(): jnp.einsum('scp,sptd->sctd', picker, block_values, preferred_element_type...]
    all_to_all x0 -> x1, blocking collectives: none -> 18.6 us  [shards(): parts = lax.all_to_all(parts, 'tensor', 0, 0)]
    ppermute x0 -> x2, waiting for transfers between devices: none -> 10.6 us  [the longest x1 10.3 us: shards(): far_queries = lax.ppermute(queries, 'pool', swap)]
    pallas_call x0 -> x4, Pallas kernels: none -> 6.42 us  [the longest x1 2.64 us: shards(): pl.pallas_call(functools.partial(pack_kernel, half), out_shape=jax.ShapeD...]
    ppermute x0 -> x2, starting transfers between devices: none -> 6.41 us  [the longest x1 3.36 us: shards(): far_queries = lax.ppermute(queries, 'pool', swap)]
    all_to_all x0 -> x1, starting transfers between devices: none -> 6.06 us  [shards(): got = lax.all_to_all(packed, 'pool', 0, 0, axis_index_groups=halves)]
  transfers between devices with their start and end apart: 3 -> 3, of which waited for: 1 -> 3; matrix products, arithmetic and copies ran while one was open for 6% -> 0% of each run, Pallas kernels for 0% -> 3%
where the time goes in v1:
time: 58.8 us; the launch traced here: 57.8 us
  blocking collectives  18.6 us (32%)
  waiting for transfers between devices  14.9 us (25%)
  starting transfers between devices  12.5 us (21%)
  Pallas kernels  6.42 us (11%)
  local copies, waits for them, and re-layouts  4.74 us (8%)
  other arithmetic  0.63 us (1%)
    all_to_all x1, blocking collectives, shards(): parts = lax.all_to_all(parts, 'tensor', 0, 0)  18.6 us
    ppermute x1, waiting for transfers between devices, shards(): far_queries = lax.ppermute(queries, 'pool', swap)  10.3 us
    all_to_all x1, starting transfers between devices, shards(): got = lax.all_to_all(packed, 'pool', 0, 0, axis_index_groups=halves)  6.06 us
    unnamed x11, local copies, waits for them, and re-layouts  4.74 us
    all_to_all x1, waiting for transfers between devices, shards(): got = lax.all_to_all(packed, 'pool', 0, 0, axis_index_groups=halves)  4.28 us
    ppermute x1, starting transfers between devices, shards(): far_queries = lax.ppermute(queries, 'pool', swap)  3.36 us
    ppermute x1, starting transfers between devices, shards(): back = lax.ppermute(back, 'pool', swap)  3.05 us
    pallas_call x1, Pallas kernels, shards(): pl.pallas_call(functools.partial(pack_kernel, half), out_shape=jax.ShapeD...  2.64 us
  transfers between devices with their start and end apart: 3, of which 3 were waited for; matrix products, arithmetic and copies ran while one was open for 0% of the time, Pallas kernels for 3%

profile of v1, /device:TPU:6, one launch (start us, length us, event | category | flops | bytes accessed | tf_op | source)
XLA Modules:
  0.0 57.8 jit_solution(12892961459094993799)
XLA Ops:
  0.0 1.3 %copy.11.owner_ref = s32[32,1]{1,0:T(8,128)} copy(s32[32,1]{0,1:T(1,128)} %param.17) | data formatting | bytes 256 | tf_op args[7]
  1.3 2.6 %pack.1 = bf16[16,272,128]{2,1,0:T(8,128)(2,1)} custom-call(s32[32,1]{1,0:T(8,128)} %copy.11.owner_ref, s32[32]{0:T(128)} %dest_ref.1, s32[32]{0:T(128)} %len_ref.1, bf16[32,32,128]{2,1,0:T(8,128)(2,1)} %keys_ref.2, bf16[32,32,128]{2,1,0:T(8,128)(2,1)} %values_ref.2), custom_call_target="tpu_custom_call" | custom-call | tf_op jit(solution)/shard_map/pack/pallas_call | solution.py:199
  4.0 0.0 copy-start.3
  4.0 0.0 copy-start.2
  4.0 6.1 %all-to-all-start = ((bf16[16,272,128]{2,1,0:T(8,128)(2,1)}), bf16[16,272,128]{2,1,0:T(8,128)(2,1)S(1)}, u32[]{:S(2)}, u32[]{:S(2)}) async-start(bf16[16,272,128]{2,1,0:T(8,128)(2,1)} %pack.1), calls=%async_computation | async-start | bytes 2228224 | tf_op jit(solution)/shard_map/all_to_all | solution.py:212
  10.0 0.0 copy-done.3
  10.1 0.0 copy-start.1
  10.1 0.0 copy-start.4
  10.1 3.4 %collective-permute-start = (bf16[16,1024]{1,0:T(8,128)(2,1)S(1)}, bf16[16,1024]{1,0:T(8,128)(2,1)S(1)}, u32[]{:S(2)}, u32[]{:S(2)}) collective-permute-start(bf16[16,1024]{1,0:T(8,128)(2,1)S(1)} %copy-done.3), channel_id=1, source_target_pairs={{0,128},{8,136},{16,144},{24,152},{32,160},{40,168},{48,176},{56,1... | collective-permute-start | bytes 98312 | tf_op jit(solution)/shard_map/ppermute | solution.py:198
  13.4 10.3 %collective-permute-done.q_ref = bf16[16,1024]{1,0:T(8,128)(2,1)S(1)} collective-permute-done((bf16[16,1024]{1,0:T(8,128)(2,1)S(1)}, bf16[16,1024]{1,0:T(8,128)(2,1)S(1)}, u32[]{:S(2)}, u32[]{:S(2)}) %collective-permute-start) | collective-permute-done | bytes 32800 | tf_op jit(solution)/shard_map/ppermute | solution.py:198
  23.8 4.3 %all-to-all-done.got_ref = bf16[16,272,128]{2,1,0:T(8,128)(2,1)S(1)} async-done(((bf16[16,272,128]{2,1,0:T(8,128)(2,1)}), bf16[16,272,128]{2,1,0:T(8,128)(2,1)S(1)}, u32[]{:S(2)}, u32[]{:S(2)}) %all-to-all-start) | async-done | bytes 1114144 | tf_op jit(solution)/shard_map/all_to_all | solution.py:212
  28.1 0.7 %partner.1 = bf16[144,128]{1,0:T(8,128)(2,1)S(1)} custom-call(bf16[16,1024]{1,0:T(8,128)(2,1)S(1)} %collective-permute-done.q_ref, bf16[16,272,128]{2,1,0:T(8,128)(2,1)S(1)} %all-to-all-done.got_ref), custom_call_target="tpu_custom_call" | custom-call | tf_op jit(solution)/shard_map/partner/pallas_call | solution.py:213
  28.8 3.0 %collective-permute-start.1 = (bf16[144,128]{1,0:T(8,128)(2,1)S(1)}, bf16[144,128]{1,0:T(8,128)(2,1)S(1)}, u32[]{:S(2)}, u32[]{:S(2)}) collective-permute-start(bf16[144,128]{1,0:T(8,128)(2,1)S(1)} %partner.1), channel_id=1, source_target_pairs={{0,128},{8,136},{16,144},{24,152},{32,160},{40,168},{48,176},{56,1... | collective-permute-start | bytes 110600 | tf_op jit(solution)/shard_map/ppermute | solution.py:222
  31.8 0.0 copy-done.2
  31.8 0.0 copy-done.1
  31.8 0.0 copy-done.4
  31.8 1.7 %main.1 = (f32[128,128]{1,0:T(8,128)S(1)}, f32[128,128]{1,0:T(8,128)S(1)}, f32[128,128]{1,0:T(8,128)S(1)}) custom-call(s32[16]{0:T(128)S(1)} %copy-done.4, bf16[16,1024]{1,0:T(8,128)(2,1)S(1)} %copy-done.3, bf16[16,256,128]{2,1,0:T(8,128)(2,1)S(1)} %copy-done.1, bf16[16,256,128]{2,1,0:T(8,128)(2,1)S(1)} %copy-done.2, ...), custom_call_target="tpu_custom_call" | custom-call | flops 200000000 | bytes 4000000 | tf_op jit(solution)/shard_map/main/pallas_call | solution.py:223
  33.5 0.3 collective-permute-done.1.back_ref
  33.8 0.0 copy-start
  33.8 3.4 %copy-done = bf16[1024,4096]{1,0:T(8,128)(2,1)S(1)} copy-done((bf16[1024,4096]{1,0:T(8,128)(2,1)S(1)}, bf16[1024,4096]{1,0:T(8,128)(2,1)}, u32[]{:S(2)}) %copy-start) | copy-done | bytes 8388632
  37.1 1.4 %project.1 = bf16[8,16,512]{2,1,0:T(8,128)(2,1)S(1)} custom-call(f32[128,128]{1,0:T(8,128)S(1)} %get-tuple-element.8.main_ref, f32[128,128]{1,0:T(8,128)S(1)} %get-tuple-element.9.top_ref, f32[128,128]{1,0:T(8,128)S(1)} %get-tuple-element.10.sum_ref, bf16[144,128]{1,0:T(8,128)(2,1)S(1)} %collective-permute-done.1.back_ref, bf16[1024,4096]{1,0:T(8,128)(2,1)S(1)} %copy-done), custom_call_target="tpu_custom_call" | custom-call | tf_op jit(solution)/shard_map/project/pallas_call | solution.py:233
  38.6 18.6 %all_to_all.10 = bf16[8,16,512]{2,1,0:T(8,128)(2,1)S(1)} all-to-all(bf16[8,16,512]{2,1,0:T(8,128)(2,1)S(1)} %project.1), channel_id=1, replica_groups=mesh['pool'=32,'tensor'=8] {'tensor'}, dimensions={0} | all-to-all | bytes 262144 | tf_op jit(solution)/shard_map/all_to_all | solution.py:242
  57.2 0.6 %reduce_sum.12 = bf16[16,512]{1,0:T(8,128)(2,1)} reduce(bf16[8,16,512]{2,1,0:T(8,128)(2,1)S(1)} %all_to_all.10, bf16[]{:T(256)} %constant.2.clone.1), dimensions={0}, to_apply=%region_0.0 | reduce | flops 57344 | bytes 147458 | tf_op jit(solution)/shard_map/reduce_sum | solution.py:243
Async XLA Ops:
  4.0 6.1 %copy-start.3 = (bf16[16,1024]{1,0:T(8,128)(2,1)S(1)}, bf16[16,1024]{1,0:T(8,128)(2,1)}, u32[]{:S(2)}) copy-start(bf16[16,1024]{1,0:T(8,128)(2,1)} %q_ref.1) | copy-start | bytes 98308
  4.0 27.8 %copy-start.2 = (bf16[16,256,128]{2,1,0:T(8,128)(2,1)S(1)}, bf16[16,256,128]{2,1,0:T(8,128)(2,1)}, u32[]{:S(2)}) copy-start(bf16[16,256,128]{2,1,0:T(8,128)(2,1)} %values_ref.3) | copy-start | bytes 3145732
  4.0 24.1 %all-to-all-start = ((bf16[16,272,128]{2,1,0:T(8,128)(2,1)}), bf16[16,272,128]{2,1,0:T(8,128)(2,1)S(1)}, u32[]{:S(2)}, u32[]{:S(2)}) async-start(bf16[16,272,128]{2,1,0:T(8,128)(2,1)} %pack.1), calls=%async_computation | async-start | bytes 2228224 | tf_op jit(solution)/shard_map/all_to_all | solution.py:212
  10.1 21.8 %copy-start.1 = (bf16[16,256,128]{2,1,0:T(8,128)(2,1)S(1)}, bf16[16,256,128]{2,1,0:T(8,128)(2,1)}, u32[]{:S(2)}) copy-start(bf16[16,256,128]{2,1,0:T(8,128)(2,1)} %keys_ref.3) | copy-start | bytes 3145732
  10.1 21.8 %copy-start.4 = (s32[16]{0:T(128)S(1)}, s32[16]{0:T(128)}, u32[]{:S(2)}) copy-start(s32[16]{0:T(128)} %lens_ref.1) | copy-start | bytes 196
  10.1 13.7 %collective-permute-start = (bf16[16,1024]{1,0:T(8,128)(2,1)S(1)}, bf16[16,1024]{1,0:T(8,128)(2,1)S(1)}, u32[]{:S(2)}, u32[]{:S(2)}) collective-permute-start(bf16[16,1024]{1,0:T(8,128)(2,1)S(1)} %copy-done.3), channel_id=1, source_target_pairs={{0,128},{8,136},{16,144},{24,152},{32,160},{40,168},{48,176},{56,1... | collective-permute-start | bytes 98312 | tf_op jit(solution)/shard_map/ppermute | solution.py:198
  28.8 5.0 %collective-permute-start.1 = (bf16[144,128]{1,0:T(8,128)(2,1)S(1)}, bf16[144,128]{1,0:T(8,128)(2,1)S(1)}, u32[]{:S(2)}, u32[]{:S(2)}) collective-permute-start(bf16[144,128]{1,0:T(8,128)(2,1)S(1)} %partner.1), channel_id=1, source_target_pairs={{0,128},{8,136},{16,144},{24,152},{32,160},{40,168},{48,176},{56,1... | collective-permute-start | bytes 110600 | tf_op jit(solution)/shard_map/ppermute | solution.py:222
  33.8 3.4 %copy-start = (bf16[1024,4096]{1,0:T(8,128)(2,1)S(1)}, bf16[1024,4096]{1,0:T(8,128)(2,1)}, u32[]{:S(2)}) copy-start(bf16[1024,4096]{1,0:T(8,128)(2,1)} %weight_ref.1) | copy-start | bytes 25165828

commit v2 on v1

--- a/solution.py
+++ b/solution.py
@@ -10,44 +10,53 @@
 
 HD = 128
 CAP = 2
+EARLY = 256
+LATE = 0
 NEG = -(2.0**99)
 VMEM = pltpu.VMEM
 SMEM = pltpu.SMEM
 NT = (((1,), (1,)), ((), ()))
 
 
-def pack_kernel(half, owner_ref, dest_ref, len_ref, keys_ref, values_ref, out_ref, count, index, length, target):
-    prompts, plen, _ = keys_ref.shape
+def pack_kernel(
+    half, owner_hbm, dest_hbm, len_hbm, keys_hbm, values_hbm, out_ref, owner_ref, dest_ref, len_ref, keys, values, sems, count, length, target
+):
+    prompts, plen, _ = keys.shape
     blocks = out_ref.shape[0]
     width = CAP * plen
+    pairs = ((owner_hbm, owner_ref), (dest_hbm, dest_ref), (len_hbm, len_ref), (keys_hbm, keys), (values_hbm, values))
+    loads = [pltpu.make_async_copy(a, b, sems.at[i]) for i, (a, b) in enumerate(pairs)]
+    for load in loads:
+        load.start()
+    zeros = jnp.zeros((width, HD), jnp.bfloat16)
+    for b in range(blocks):
+        out_ref[b, width : 2 * width, :] = zeros
+        out_ref[b, 3 * width : 4 * width, :] = zeros
     my_half = lax.axis_index("pool") // half
     for i in range(2 * half):
         count[i] = 0
     for i in range(blocks * 2 * CAP):
-        index[i] = 0
         length[i] = 0
         target[i] = 0
+    for load in loads[:3]:
+        load.wait()
+    places = []
     for p in range(prompts):
-        group = owner_ref[p, 0]
-        rank = count[group]
+        group = owner_ref[p]
+        rank = jnp.minimum(count[group], CAP - 1)
         count[group] = rank + 1
+        block = group % half
         other = jnp.where(group // half == my_half, 0, 1)
-        slot = (group % half) * (2 * CAP) + other * CAP + jnp.minimum(rank, CAP - 1)
-        index[slot] = p
+        slot = block * (2 * CAP) + other * CAP + rank
         length[slot] = len_ref[p]
         target[slot] = dest_ref[p]
+        places.append((block, other * 2 * width + rank * plen))
     row = lax.broadcasted_iota(jnp.int32, (16, 128), 0)
     lane = lax.broadcasted_iota(jnp.int32, (16, 128), 1)
     pos = lane % plen
     second = (lane // plen) % CAP == 1
     lower = row < 8
     for b in range(blocks):
-        for other in range(2):
-            for r in range(CAP):
-                p = index[b * 2 * CAP + other * CAP + r]
-                at = other * 2 * width + r * plen
-                out_ref[b, at : at + plen, :] = keys_ref[p]
-                out_ref[b, at + width : at + width + plen, :] = values_ref[p]
         s = b * 2 * CAP
         limit = jnp.where(
             lower,
@@ -61,6 +70,11 @@
         )
         code = jnp.where(pos < limit, code, -1)
         out_ref[b, 4 * width :, :] = code.astype(jnp.float32).astype(jnp.bfloat16)
+    for load in loads[3:]:
+        load.wait()
+    for p, (block, at) in enumerate(places):
+        out_ref[block, pl.ds(pl.multiple_of(at, plen), plen), :] = keys[p]
+        out_ref[block, pl.ds(pl.multiple_of(at + width, plen), plen), :] = values[p]
 
 
 def split_heads(q_ref, scratch):
@@ -115,34 +129,46 @@
     out_ref[rows:, :] = jnp.transpose(stats)[:16, :].astype(jnp.bfloat16)
 
 
-def main_kernel(scale, lens_ref, q_ref, keys_ref, values_ref, got_ref, out_ref, top_ref, sum_ref, scratch):
+def cache_kernel(scale, lens_ref, q_ref, keys_ref, values_ref, weight_hbm, out_ref, top_ref, sum_ref, q_out_ref, weight_ref, scratch, sem):
+    load = pltpu.make_async_copy(weight_hbm.at[:EARLY], weight_ref, sem)
+    load.start()
     seqs, ctx, _ = keys_ref.shape
     rows = split_heads(q_ref, scratch)
-    q = jnp.concatenate(rows, axis=0).astype(jnp.bfloat16)
-    heads = q.shape[0] // seqs
+    q_out_ref[...] = jnp.concatenate(rows, axis=0)
+    heads = rows[0].shape[0]
     col = lax.broadcasted_iota(jnp.int32, (heads, ctx), 1)
-    cache = []
+    scores = []
     for s in range(seqs):
         sc = lax.dot_general(rows[s].astype(jnp.bfloat16), keys_ref[s], NT, preferred_element_type=jnp.float32)
-        cache.append(jnp.where(col < lens_ref[s], sc * scale, NEG))
-    scores = prompt_scores(q, got_ref, 0, scale)
-    cache_all = jnp.concatenate(cache, axis=0)
-    top = functools.reduce(jnp.maximum, scores + [cache_all[:, i : i + 128] for i in range(0, ctx, 128)])
-    top = jnp.max(top, axis=1, keepdims=True)
-    cache_exp = jnp.exp(cache_all - top)
-    exps = [jnp.exp(s - top) for s in scores]
-    total = functools.reduce(jnp.add, exps + [cache_exp[:, i : i + 128] for i in range(0, ctx, 128)])
-    total = jnp.sum(total, axis=1, keepdims=True)
-    parts = []
+        scores.append(jnp.where(col < lens_ref[s], sc * scale, NEG))
+    scores = jnp.concatenate(scores, axis=0)
+    top = jnp.max(scores, axis=1, keepdims=True)
+    exps = jnp.exp(scores - top)
+    total = jnp.sum(exps, axis=1, keepdims=True)
     for s in range(seqs):
-        w = cache_exp[s * heads : (s + 1) * heads].astype(jnp.bfloat16)
-        parts.append(jnp.dot(w, values_ref[s], preferred_element_type=jnp.float32))
-    out_ref[...] = jnp.concatenate(parts, axis=0) + prompt_sum(exps, got_ref, 0)
+        w = exps[s * heads : (s + 1) * heads].astype(jnp.bfloat16)
+        out_ref[s * heads : (s + 1) * heads, :] = jnp.dot(w, values_ref[s], preferred_element_type=jnp.float32)
     top_ref[...] = jnp.broadcast_to(top, top_ref.shape)
     sum_ref[...] = jnp.broadcast_to(total, sum_ref.shape)
-
-
-def project_kernel(main_ref, top_ref, sum_ref, back_ref, weight_ref, out_ref, scratch):
+    load.wait()
+
+
+def own_kernel(scale, q_ref, got_ref, cache_ref, cache_top_ref, cache_sum_ref, weight_hbm, out_ref, top_ref, sum_ref, weight_ref, sem):
+    load = pltpu.make_async_copy(weight_hbm.at[EARLY : weight_hbm.shape[0] - LATE], weight_ref, sem)
+    load.start()
+    scores = prompt_scores(q_ref[...].astype(jnp.bfloat16), got_ref, 0, scale)
+    top = jnp.max(functools.reduce(jnp.maximum, scores), axis=1, keepdims=True)
+    top = jnp.maximum(top, cache_top_ref[...])
+    exps = [jnp.exp(s - top) for s in scores]
+    total = jnp.sum(functools.reduce(jnp.add, exps), axis=1, keepdims=True)
+    near = jnp.exp(cache_top_ref[...] - top)
+    out_ref[...] = prompt_sum(exps, got_ref, 0) + cache_ref[...] * near
+    top_ref[...] = top
+    sum_ref[...] = total + cache_sum_ref[...] * near
+    load.wait()
+
+
+def project_kernel(main_ref, top_ref, sum_ref, back_ref, weight0_ref, weight1_ref, out_ref, scratch):
     pieces, seqs, cols = out_ref.shape
     rows = main_ref.shape[0]
     heads = rows // seqs
@@ -158,9 +184,18 @@
     attended = jnp.concatenate(
         [scratch[pl.ds(h, seqs, stride=heads), :].astype(jnp.bfloat16) for h in range(heads)], axis=1
     )
+    parts = [0.0] * pieces
+    at = 0
     for c in range(pieces):
-        part = jnp.dot(attended, weight_ref[:, c * cols : (c + 1) * cols], preferred_element_type=jnp.float32)
-        out_ref[c] = part.astype(out_ref.dtype)
+        w = weight0_ref[:, c * cols : (c + 1) * cols]
+        parts[c] += jnp.dot(attended[:, at : at + w.shape[0]], w, preferred_element_type=jnp.float32)
+    at += weight0_ref.shape[0]
+    for c in range(pieces):
+        w = weight1_ref[:, c * cols : (c + 1) * cols]
+        parts[c] += jnp.dot(attended[:, at : at + w.shape[0]], w, preferred_element_type=jnp.float32)
+    at += weight1_ref.shape[0]
+    for c in range(pieces):
+        out_ref[c] = parts[c].astype(out_ref.dtype)
 
 
 def vmem(n):
@@ -195,50 +230,63 @@
     scale = 1.0 / math.sqrt(HD)
     swap = [(i, (i + half) % pool) for i in range(pool)]
     halves = [list(range(half)), list(range(half, pool))]
+    in_hbm = lambda x: pltpu.with_memory_space_constraint(x, pltpu.HBM)
+    anywhere = pl.BlockSpec(memory_space=pltpu.HBM)
+    small = VMEM((rows, HD), jnp.float32)
     far_queries = lax.ppermute(queries, "pool", swap)
     packed = pl.pallas_call(
         functools.partial(pack_kernel, half),
         out_shape=jax.ShapeDtypeStruct((half, 4 * width + 16, HD), jnp.bfloat16),
-        in_specs=smem(3) + vmem(2),
+        in_specs=[anywhere] * 5,
         out_specs=pl.BlockSpec(memory_space=VMEM),
-        scratch_shapes=[
-            SMEM((pool,), jnp.int32),
-            SMEM((half * 2 * CAP,), jnp.int32),
-            SMEM((half * 2 * CAP,), jnp.int32),
-            SMEM((half * 2 * CAP,), jnp.int32),
-        ],
+        scratch_shapes=[SMEM((prompts,), jnp.int32)] * 3
+        + [VMEM((prompts, plen, HD), jnp.bfloat16)] * 2
+        + [pltpu.SemaphoreType.DMA((5,)), SMEM((pool,), jnp.int32)]
+        + [SMEM((half * 2 * CAP,), jnp.int32)] * 2,
+        compiler_params=pltpu.CompilerParams(vmem_limit_bytes=16 << 20),
         name="pack",
-    )(matching, dest_seq, prompt_lens, prompt_keys, prompt_values)
+    )(*[in_hbm(x) for x in (matching.reshape(-1), dest_seq, prompt_lens, prompt_keys, prompt_values)])
     got = lax.all_to_all(packed, "pool", 0, 0, axis_index_groups=halves)
+    cache, cache_top, cache_sum, heads_first, weight0 = pl.pallas_call(
+        functools.partial(cache_kernel, scale),
+        out_shape=[jax.ShapeDtypeStruct((rows, HD), jnp.float32)] * 4 + [VMEM((EARLY, out_cols), out_weight.dtype)],
+        in_specs=smem(1) + vmem(3) + [anywhere],
+        out_specs=vmem(5),
+        scratch_shapes=[small, pltpu.SemaphoreType.DMA],
+        compiler_params=pltpu.CompilerParams(vmem_limit_bytes=24 << 20),
+        cost_estimate=pl.CostEstimate(flops=200_000_000, bytes_accessed=12_000_000, transcendentals=200_000),
+        name="cache",
+    )(*[in_hbm(x) for x in (context_lens, queries, cache_keys, cache_values, out_weight)])
+    far_queries, cache = lax.optimization_barrier((far_queries, cache))
     back = pl.pallas_call(
         functools.partial(partner_kernel, scale),
         out_shape=jax.ShapeDtypeStruct((rows + 16, HD), jnp.bfloat16),
         in_specs=vmem(2),
         out_specs=pl.BlockSpec(memory_space=VMEM),
-        scratch_shapes=[VMEM((rows, HD), jnp.float32)],
+        scratch_shapes=[small],
         compiler_params=pltpu.CompilerParams(vmem_limit_bytes=16 << 20),
         name="partner",
     )(far_queries, got)
     back = lax.ppermute(back, "pool", swap)
-    main, top, total = pl.pallas_call(
-        functools.partial(main_kernel, scale),
-        out_shape=[jax.ShapeDtypeStruct((rows, HD), jnp.float32)] * 3,
-        in_specs=smem(1) + vmem(4),
-        out_specs=vmem(3),
-        scratch_shapes=[VMEM((rows, HD), jnp.float32)],
-        compiler_params=pltpu.CompilerParams(vmem_limit_bytes=24 << 20),
-        cost_estimate=pl.CostEstimate(flops=200_000_000, bytes_accessed=4_000_000, transcendentals=200_000),
-        name="main",
-    )(context_lens, queries, cache_keys, cache_values, got)
+    main, top, total, weight = pl.pallas_call(
+        functools.partial(own_kernel, scale),
+        out_shape=[jax.ShapeDtypeStruct((rows, HD), jnp.float32)] * 3 + [VMEM((out_weight.shape[0] - EARLY - LATE, out_cols), out_weight.dtype)],
+        in_specs=vmem(5) + [anywhere],
+        out_specs=vmem(4),
+        scratch_shapes=[pltpu.SemaphoreType.DMA],
+        compiler_params=pltpu.CompilerParams(vmem_limit_bytes=16 << 20),
+        cost_estimate=pl.CostEstimate(flops=100_000_000, bytes_accessed=2_000_000, transcendentals=200_000),
+        name="own",
+    )(heads_first, got, cache, cache_top, cache_sum, in_hbm(out_weight))
     parts = pl.pallas_call(
         project_kernel,
         out_shape=jax.ShapeDtypeStruct((pieces, seqs, out_cols // pieces), jnp.bfloat16),
-        in_specs=vmem(5),
+        in_specs=vmem(6),
         out_specs=pl.BlockSpec(memory_space=VMEM),
-        scratch_shapes=[VMEM((rows, HD), jnp.float32)],
+        scratch_shapes=[small],
         compiler_params=pltpu.CompilerParams(vmem_limit_bytes=24 << 20),
         name="project",
-    )(main, top, total, back, out_weight)
+    )(main, top, total, back, weight0, weight)
     parts = lax.all_to_all(parts, "tensor", 0, 0)
     return jnp.sum(parts.astype(jnp.float32), axis=0).astype(jnp.bfloat16)
 

time: 58.8 us -> 53.7 us (0.913)
  local copies, waits for them, and re-layouts: 4.74 us -> 0.01 us
  Pallas kernels: 6.42 us -> 10.5 us
  waiting for transfers between devices: 14.9 us -> 11.4 us
  blocking collectives: 18.6 us -> 17.8 us
    unnamed x11 -> x2, local copies, waits for them, and re-layouts: 4.74 us -> 0.01 us
    pallas_call x1 -> x2, Pallas kernels: 1.67 us -> 6.04 us  [the longest x1 3.24 us: shards(): pl.pallas_call(functools.partial(cache_kernel, scale), out_shape=[jax.Sha...]
    ppermute x1, waiting for transfers between devices: 10.3 us -> 7.11 us  [shards(): far_queries = lax.ppermute(queries, 'pool', swap)]
    all_to_all x1, blocking collectives: 18.6 us -> 17.8 us  [shards(): parts = lax.all_to_all(parts, 'tensor', 0, 0)]
  transfers between devices with their start and end apart: 3 -> 3, of which waited for: 3 -> 2; matrix products, arithmetic and copies ran while one was open for 0% -> 0% of each run, Pallas kernels for 3% -> 11%
where the time goes in v2:
time: 53.7 us; the launch traced here: 52.7 us
  blocking collectives  17.8 us (33%)
  starting transfers between devices  12.3 us (23%)
  waiting for transfers between devices  11.4 us (21%)
  Pallas kernels  10.5 us (20%)
  other arithmetic  0.63 us (1%)
    all_to_all x1, blocking collectives, shards(): parts = lax.all_to_all(parts, 'tensor', 0, 0)  17.8 us
    ppermute x1, waiting for transfers between devices, shards(): far_queries = lax.ppermute(queries, 'pool', swap)  7.11 us
    all_to_all x1, starting transfers between devices, shards(): got = lax.all_to_all(packed, 'pool', 0, 0, axis_index_groups=halves)  5.94 us
    all_to_all x1, waiting for transfers between devices, shards(): got = lax.all_to_all(packed, 'pool', 0, 0, axis_index_groups=halves)  4.28 us
    ppermute x1, starting transfers between devices, shards(): far_queries = lax.ppermute(queries, 'pool', swap)  3.36 us
    pallas_call x1, Pallas kernels, shards(): pl.pallas_call(functools.partial(cache_kernel, scale), out_shape=[jax.Sha...  3.24 us
    ppermute x1, starting transfers between devices, shards(): back = lax.ppermute(back, 'pool', swap)  3.05 us
    pallas_call x1, Pallas kernels, shards(): pl.pallas_call(functools.partial(own_kernel, scale), out_shape=[jax.Shape...  2.79 us
  transfers between devices with their start and end apart: 3, of which 2 were waited for; matrix products, arithmetic and copies ran while one was open for 0% of the time, Pallas kernels for 11%

profile of v2, /device:TPU:6, one launch (start us, length us, event | category | flops | bytes accessed | tf_op | source)
XLA Modules:
  0.0 52.7 jit_solution(13228030212743134292)
XLA Ops:
  0.0 0.0 copy-start
  0.0 2.4 %pack.1 = bf16[16,272,128]{2,1,0:T(8,128)(2,1)} custom-call(s32[32]{0:T(128)} %bitcast.1, s32[32]{0:T(128)} %dest_hbm.1, s32[32]{0:T(128)} %len_hbm.1, bf16[32,32,128]{2,1,0:T(8,128)(2,1)} %keys_hbm.1, bf16[32,32,128]{2,1,0:T(8,128)(2,1)} %values_hbm.1), custom_call_target="tpu_custom_call" | custom-call | tf_op jit(solution)/shard_map/pack/pallas_call | solution.py:237
  2.4 5.9 %all-to-all-start = ((bf16[16,272,128]{2,1,0:T(8,128)(2,1)}), bf16[16,272,128]{2,1,0:T(8,128)(2,1)S(1)}, u32[]{:S(2)}, u32[]{:S(2)}) async-start(bf16[16,272,128]{2,1,0:T(8,128)(2,1)} %pack.1), calls=%async_computation | async-start | bytes 2228224 | tf_op jit(solution)/shard_map/all_to_all | solution.py:249
  8.3 0.0 copy-done
  8.3 3.4 %collective-permute-start = (bf16[16,1024]{1,0:T(8,128)(2,1)S(1)}, bf16[16,1024]{1,0:T(8,128)(2,1)S(1)}, u32[]{:S(2)}, u32[]{:S(2)}) collective-permute-start(bf16[16,1024]{1,0:T(8,128)(2,1)S(1)} %copy-done), channel_id=1, source_target_pairs={{0,128},{8,136},{16,144},{24,152},{32,160},{40,168},{48,176},{56,1... | collective-permute-start | bytes 98312 | tf_op jit(solution)/shard_map/ppermute | solution.py:236
  11.7 3.2 %cache.1 = (f32[128,128]{1,0:T(8,128)S(1)}, f32[128,128]{1,0:T(8,128)S(1)}, f32[128,128]{1,0:T(8,128)S(1)}, f32[128,128]{1,0:T(8,128)S(1)}, bf16[256,4096]{1,0:T(8,128)(2,1)S(1)}) custom-call(s32[16]{0:T(128)} %lens_ref.1, bf16[16,1024]{1,0:T(8,128)(2,1)} %q_ref.1, bf16[16,256,128]{2,1,0:T(8,128)(2,1)} %keys_ref.1, bf16[16,256,128]{2,1,0:T(8,128)(2,1)} %values_ref.1, ...), custom_call_target="tpu_custom_call" | custom-call | flops 200000000 | bytes 12000000 | tf_op jit(solution)/shard_map/cache/pallas_call | solution.py:250
  15.0 7.1 %collective-permute-done.q_ref = bf16[16,1024]{1,0:T(8,128)(2,1)S(1)} collective-permute-done((bf16[16,1024]{1,0:T(8,128)(2,1)S(1)}, bf16[16,1024]{1,0:T(8,128)(2,1)S(1)}, u32[]{:S(2)}, u32[]{:S(2)}) %collective-permute-start) | collective-permute-done | bytes 32800 | tf_op jit(solution)/shard_map/ppermute | solution.py:236
  22.1 4.3 %all-to-all-done.got_ref = bf16[16,272,128]{2,1,0:T(8,128)(2,1)S(1)} async-done(((bf16[16,272,128]{2,1,0:T(8,128)(2,1)}), bf16[16,272,128]{2,1,0:T(8,128)(2,1)S(1)}, u32[]{:S(2)}, u32[]{:S(2)}) %all-to-all-start) | async-done | bytes 1114144 | tf_op jit(solution)/shard_map/all_to_all | solution.py:249
  26.4 0.7 %partner.1 = bf16[144,128]{1,0:T(8,128)(2,1)S(1)} custom-call(bf16[16,1024]{1,0:T(8,128)(2,1)S(1)} %collective-permute-done.q_ref, bf16[16,272,128]{2,1,0:T(8,128)(2,1)S(1)} %all-to-all-done.got_ref), custom_call_target="tpu_custom_call" | custom-call | tf_op jit(solution)/shard_map/partner/pallas_call | solution.py:261
  27.1 3.1 %collective-permute-start.1 = (bf16[144,128]{1,0:T(8,128)(2,1)S(1)}, bf16[144,128]{1,0:T(8,128)(2,1)S(1)}, u32[]{:S(2)}, u32[]{:S(2)}) collective-permute-start(bf16[144,128]{1,0:T(8,128)(2,1)S(1)} %partner.1), channel_id=1, source_target_pairs={{0,128},{8,136},{16,144},{24,152},{32,160},{40,168},{48,176},{56,1... | collective-permute-start | bytes 110600 | tf_op jit(solution)/shard_map/ppermute | solution.py:270
  30.1 2.8 %own.1 = (f32[128,128]{1,0:T(8,128)S(1)}, f32[128,128]{1,0:T(8,128)S(1)}, f32[128,128]{1,0:T(8,128)S(1)}, bf16[768,4096]{1,0:T(8,128)(2,1)S(1)}) custom-call(f32[128,128]{1,0:T(8,128)S(1)} %get-tuple-element.16.q_ref, bf16[16,272,128]{2,1,0:T(8,128)(2,1)S(1)} %all-to-all-done.got_ref, f32[128,128]{1,0:T(8,128)S(1)} %get-tuple-element.18.cache_ref, ...), custom_call_target="tpu_custom_call" | custom-call | flops 100000000 | bytes 2000000 | tf_op jit(solution)/shard_map/own/pallas_call | solution.py:271
  32.9 0.0 collective-permute-done.1.back_ref
  32.9 1.4 %project.1 = bf16[8,16,512]{2,1,0:T(8,128)(2,1)S(1)} custom-call(f32[128,128]{1,0:T(8,128)S(1)} %get-tuple-element.21.main_ref, f32[128,128]{1,0:T(8,128)S(1)} %get-tuple-element.22.top_ref, f32[128,128]{1,0:T(8,128)S(1)} %get-tuple-element.23.sum_ref, bf16[144,128]{1,0:T(8,128)(2,1)S(1)} %collective-permute-done.1.back_ref, ...), custom_call_target="tpu_custom_call" | custom-call | tf_op jit(solution)/shard_map/project/pallas_call | solution.py:281
  34.3 17.8 %all_to_all.10 = bf16[8,16,512]{2,1,0:T(8,128)(2,1)S(1)} all-to-all(bf16[8,16,512]{2,1,0:T(8,128)(2,1)S(1)} %project.1), channel_id=1, replica_groups=mesh['pool'=32,'tensor'=8] {'tensor'}, dimensions={0} | all-to-all | bytes 262144 | tf_op jit(solution)/shard_map/all_to_all | solution.py:290
  52.1 0.6 %reduce_sum.12 = bf16[16,512]{1,0:T(8,128)(2,1)} reduce(bf16[8,16,512]{2,1,0:T(8,128)(2,1)S(1)} %all_to_all.10, bf16[]{:T(256)} %constant.2.clone.1), dimensions={0}, to_apply=%region_0.0 | reduce | flops 57344 | bytes 147458 | tf_op jit(solution)/shard_map/reduce_sum | solution.py:291
Async XLA Ops:
  0.0 8.3 %copy-start = (bf16[16,1024]{1,0:T(8,128)(2,1)S(1)}, bf16[16,1024]{1,0:T(8,128)(2,1)}, u32[]{:S(2)}) copy-start(bf16[16,1024]{1,0:T(8,128)(2,1)} %q_ref.1) | copy-start | bytes 98308
  2.4 24.0 %all-to-all-start = ((bf16[16,272,128]{2,1,0:T(8,128)(2,1)}), bf16[16,272,128]{2,1,0:T(8,128)(2,1)S(1)}, u32[]{:S(2)}, u32[]{:S(2)}) async-start(bf16[16,272,128]{2,1,0:T(8,128)(2,1)} %pack.1), calls=%async_computation | async-start | bytes 2228224 | tf_op jit(solution)/shard_map/all_to_all | solution.py:249
  8.3 13.7 %collective-permute-start = (bf16[16,1024]{1,0:T(8,128)(2,1)S(1)}, bf16[16,1024]{1,0:T(8,128)(2,1)S(1)}, u32[]{:S(2)}, u32[]{:S(2)}) collective-permute-start(bf16[16,1024]{1,0:T(8,128)(2,1)S(1)} %copy-done), channel_id=1, source_target_pairs={{0,128},{8,136},{16,144},{24,152},{32,160},{40,168},{48,176},{56,1... | collective-permute-start | bytes 98312 | tf_op jit(solution)/shard_map/ppermute | solution.py:236
  27.1 5.9 %collective-permute-start.1 = (bf16[144,128]{1,0:T(8,128)(2,1)S(1)}, bf16[144,128]{1,0:T(8,128)(2,1)S(1)}, u32[]{:S(2)}, u32[]{:S(2)}) collective-permute-start(bf16[144,128]{1,0:T(8,128)(2,1)S(1)} %partner.1), channel_id=1, source_target_pairs={{0,128},{8,136},{16,144},{24,152},{32,160},{40,168},{48,176},{56,1... | collective-permute-start | bytes 110600 | tf_op jit(solution)/shard_map/ppermute | solution.py:270

commit v3 on v2

--- a/solution.py
+++ b/solution.py
@@ -32,7 +32,8 @@
     for b in range(blocks):
         out_ref[b, width : 2 * width, :] = zeros
         out_ref[b, 3 * width : 4 * width, :] = zeros
-    my_half = lax.axis_index("pool") // half
+    bits = half.bit_length() - 1
+    my_half = lax.axis_index("pool") >> bits
     for i in range(2 * half):
         count[i] = 0
     for i in range(blocks * 2 * CAP):
@@ -45,8 +46,8 @@
         group = owner_ref[p]
         rank = jnp.minimum(count[group], CAP - 1)
         count[group] = rank + 1
-        block = group % half
-        other = jnp.where(group // half == my_half, 0, 1)
+        block = group & (half - 1)
+        other = (group >> bits) ^ my_half
         slot = block * (2 * CAP) + other * CAP + rank
         length[slot] = len_ref[p]
         target[slot] = dest_ref[p]
@@ -287,8 +288,16 @@
         compiler_params=pltpu.CompilerParams(vmem_limit_bytes=24 << 20),
         name="project",
     )(main, top, total, back, weight0, weight)
-    parts = lax.all_to_all(parts, "tensor", 0, 0)
-    return jnp.sum(parts.astype(jnp.float32), axis=0).astype(jnp.bfloat16)
+    second = lax.axis_index("tensor") % 2 == 1
+    ring = [[i for i in range(pieces) if i % 2 == k] for k in range(2)]
+    parts, second = lax.optimization_barrier((parts, second))
+    parts = parts.reshape(pieces // 2, 2, seqs, out_cols // pieces)
+    parts = lax.all_to_all(parts, "tensor", 0, 0, axis_index_groups=ring)
+    parts = jnp.sum(parts.astype(jnp.float32), axis=0)
+    away = jnp.where(second, parts[0], parts[1]).astype(jnp.bfloat16)
+    near = jnp.where(second, parts[1], parts[0])
+    away = lax.ppermute(away, "tensor", [(i, i ^ 1) for i in range(pieces)])
+    return (near + away.astype(jnp.float32)).astype(jnp.bfloat16)
 
 
 def solution(mesh):

time: 53.7 us -> 52 us (0.968)
  blocking collectives: 17.8 us -> 8.48 us
  starting transfers between devices: 12.3 us -> 17.8 us
  waiting for transfers between devices: 11.4 us -> 13.6 us
    all_to_all x1, blocking collectives: 17.8 us -> 8.48 us  [shards(): parts = lax.all_to_all(parts, 'tensor', 0, 0, axis_index_groups=ring)]
    ppermute x0 -> x1, starting transfers between devices: none -> 5.49 us  [shards(): away = lax.ppermute(away, 'tensor', [(i, i ^ 1) for i in range(pieces)])]
    ppermute x0 -> x1, waiting for transfers between devices: none -> 2.24 us  [shards(): away = lax.ppermute(away, 'tensor', [(i, i ^ 1) for i in range(pieces)])]
    convert_element_type x0 -> x2, other arithmetic: none -> 0.62 us  [the longest x1 0.61 us: shards(): return (near + away.astype(jnp.float32)).astype(jnp.bfloat16)]
    reduce_sum x1, other arithmetic: 0.63 us -> 0.02 us  [shards(): parts = jnp.sum(parts.astype(jnp.float32), axis=0)]
  transfers between devices with their start and end apart: 3 -> 4, of which waited for: 2 -> 3; matrix products, arithmetic and copies ran while one was open for 0% -> 0% of each run, Pallas kernels for 11% -> 12%
where the time goes in v3:
time: 52 us; the launch traced here: 51 us
  starting transfers between devices  17.8 us (34%)
  waiting for transfers between devices  13.6 us (26%)
  Pallas kernels  10.4 us (20%)
  blocking collectives  8.48 us (16%)
  other arithmetic  0.64 us (1%)
    all_to_all x1, blocking collectives, shards(): parts = lax.all_to_all(parts, 'tensor', 0, 0, axis_index_groups=ring)  8.48 us
    ppermute x1, waiting for transfers between devices, shards(): far_queries = lax.ppermute(queries, 'pool', swap)  7.11 us
    all_to_all x1, starting transfers between devices, shards(): got = lax.all_to_all(packed, 'pool', 0, 0, axis_index_groups=halves)  5.94 us
    ppermute x1, starting transfers between devices, shards(): away = lax.ppermute(away, 'tensor', [(i, i ^ 1) for i in range(pieces)])  5.49 us
    all_to_all x1, waiting for transfers between devices, shards(): got = lax.all_to_all(packed, 'pool', 0, 0, axis_index_groups=halves)  4.28 us
    ppermute x1, starting transfers between devices, shards(): far_queries = lax.ppermute(queries, 'pool', swap)  3.36 us
    pallas_call x1, Pallas kernels, shards(): pl.pallas_call(functools.partial(cache_kernel, scale), out_shape=[jax.Sha...  3.24 us
    ppermute x1, starting transfers between devices, shards(): back = lax.ppermute(back, 'pool', swap)  3.05 us
  transfers between devices with their start and end apart: 4, of which 3 were waited for; matrix products, arithmetic and copies ran while one was open for 0% of the time, Pallas kernels for 12%

profile of v3, /device:TPU:6, one launch (start us, length us, event | category | flops | bytes accessed | tf_op | source)
XLA Modules:
  0.0 51.0 jit_solution(13690721662674780570)
XLA Ops:
  0.0 0.0 copy-start
  0.0 2.2 %pack.1 = bf16[16,272,128]{2,1,0:T(8,128)(2,1)} custom-call(s32[32]{0:T(128)} %bitcast.9, s32[32]{0:T(128)} %dest_hbm.1, s32[32]{0:T(128)} %len_hbm.1, bf16[32,32,128]{2,1,0:T(8,128)(2,1)} %keys_hbm.1, bf16[32,32,128]{2,1,0:T(8,128)(2,1)} %values_hbm.1), custom_call_target="tpu_custom_call" | custom-call | tf_op jit(solution)/shard_map/pack/pallas_call | solution.py:238
  2.2 5.9 %all-to-all-start = ((bf16[16,272,128]{2,1,0:T(8,128)(2,1)}), bf16[16,272,128]{2,1,0:T(8,128)(2,1)S(1)}, u32[]{:S(2)}, u32[]{:S(2)}) async-start(bf16[16,272,128]{2,1,0:T(8,128)(2,1)} %pack.1), calls=%async_computation | async-start | bytes 2228224 | tf_op jit(solution)/shard_map/all_to_all | solution.py:250
  8.2 0.0 copy-done
  8.2 3.4 %collective-permute-start = (bf16[16,1024]{1,0:T(8,128)(2,1)S(1)}, bf16[16,1024]{1,0:T(8,128)(2,1)S(1)}, u32[]{:S(2)}, u32[]{:S(2)}) collective-permute-start(bf16[16,1024]{1,0:T(8,128)(2,1)S(1)} %copy-done), channel_id=1, source_target_pairs={{0,128},{8,136},{16,144},{24,152},{32,160},{40,168},{48,176},{56,1... | collective-permute-start | bytes 98312 | tf_op jit(solution)/shard_map/ppermute | solution.py:237
  11.5 3.2 %cache.1 = (f32[128,128]{1,0:T(8,128)S(1)}, f32[128,128]{1,0:T(8,128)S(1)}, f32[128,128]{1,0:T(8,128)S(1)}, f32[128,128]{1,0:T(8,128)S(1)}, bf16[256,4096]{1,0:T(8,128)(2,1)S(1)}) custom-call(s32[16]{0:T(128)} %lens_ref.1, bf16[16,1024]{1,0:T(8,128)(2,1)} %q_ref.1, bf16[16,256,128]{2,1,0:T(8,128)(2,1)} %keys_ref.1, bf16[16,256,128]{2,1,0:T(8,128)(2,1)} %values_ref.1, ...), custom_call_target="tpu_custom_call" | custom-call | flops 200000000 | bytes 12000000 | tf_op jit(solution)/shard_map/cache/pallas_call | solution.py:251
  14.8 7.1 %collective-permute-done.q_ref = bf16[16,1024]{1,0:T(8,128)(2,1)S(1)} collective-permute-done((bf16[16,1024]{1,0:T(8,128)(2,1)S(1)}, bf16[16,1024]{1,0:T(8,128)(2,1)S(1)}, u32[]{:S(2)}, u32[]{:S(2)}) %collective-permute-start) | collective-permute-done | bytes 32800 | tf_op jit(solution)/shard_map/ppermute | solution.py:237
  21.9 4.3 %all-to-all-done.got_ref = bf16[16,272,128]{2,1,0:T(8,128)(2,1)S(1)} async-done(((bf16[16,272,128]{2,1,0:T(8,128)(2,1)}), bf16[16,272,128]{2,1,0:T(8,128)(2,1)S(1)}, u32[]{:S(2)}, u32[]{:S(2)}) %all-to-all-start) | async-done | bytes 1114144 | tf_op jit(solution)/shard_map/all_to_all | solution.py:250
  26.2 0.7 %partner.1 = bf16[144,128]{1,0:T(8,128)(2,1)S(1)} custom-call(bf16[16,1024]{1,0:T(8,128)(2,1)S(1)} %collective-permute-done.q_ref, bf16[16,272,128]{2,1,0:T(8,128)(2,1)S(1)} %all-to-all-done.got_ref), custom_call_target="tpu_custom_call" | custom-call | tf_op jit(solution)/shard_map/partner/pallas_call | solution.py:262
  26.9 3.0 %collective-permute-start.1 = (bf16[144,128]{1,0:T(8,128)(2,1)S(1)}, bf16[144,128]{1,0:T(8,128)(2,1)S(1)}, u32[]{:S(2)}, u32[]{:S(2)}) collective-permute-start(bf16[144,128]{1,0:T(8,128)(2,1)S(1)} %partner.1), channel_id=1, source_target_pairs={{0,128},{8,136},{16,144},{24,152},{32,160},{40,168},{48,176},{56,1... | collective-permute-start | bytes 110600 | tf_op jit(solution)/shard_map/ppermute | solution.py:271
  29.9 2.8 %own.1 = (f32[128,128]{1,0:T(8,128)S(1)}, f32[128,128]{1,0:T(8,128)S(1)}, f32[128,128]{1,0:T(8,128)S(1)}, bf16[768,4096]{1,0:T(8,128)(2,1)S(1)}) custom-call(f32[128,128]{1,0:T(8,128)S(1)} %get-tuple-element.18.q_ref, bf16[16,272,128]{2,1,0:T(8,128)(2,1)S(1)} %all-to-all-done.got_ref, f32[128,128]{1,0:T(8,128)S(1)} %get-tuple-element.20.cache_ref, ...), custom_call_target="tpu_custom_call" | custom-call | flops 100000000 | bytes 2000000 | tf_op jit(solution)/shard_map/own/pallas_call | solution.py:272
  32.7 0.0 collective-permute-done.1.back_ref
  32.8 1.4 %project.1 = bf16[8,16,512]{2,1,0:T(8,128)(2,1)S(1)} custom-call(f32[128,128]{1,0:T(8,128)S(1)} %get-tuple-element.23.main_ref, f32[128,128]{1,0:T(8,128)S(1)} %get-tuple-element.24.top_ref, f32[128,128]{1,0:T(8,128)S(1)} %get-tuple-element.25.sum_ref, bf16[144,128]{1,0:T(8,128)(2,1)S(1)} %collective-permute-done.1.back_ref, ...), custom_call_target="tpu_custom_call" | custom-call | tf_op jit(solution)/shard_map/project/pallas_call | solution.py:282
  34.2 8.5 %all_to_all.10 = bf16[4,2,16,512]{3,2,1,0:T(8,128)(2,1)S(1)} all-to-all(bf16[4,2,16,512]{3,2,1,0:T(8,128)(2,1)S(1)} %bitcast.8), channel_id=1, replica_groups={{0,2,4,6},{1,3,5,7},{8,10,12,14},{9,11,13,15},{16,18,20,22},{17,19,21,2..., dimensions={0} | all-to-all | bytes 262144 | tf_op jit(solution)/shard_map/all_to_all | solution.py:295
  42.7 5.5 %collective-permute-start.2 = (bf16[16,512]{1,0:T(8,128)(2,1)S(1)}, bf16[16,512]{1,0:T(8,128)(2,1)S(1)}, u32[]{:S(2)}, u32[]{:S(2)}) collective-permute-start(bf16[16,512]{1,0:T(8,128)(2,1)S(1)} %fusion.1), channel_id=1, source_target_pairs={{0,1},{1,0},{2,3},{3,2},{4,5},{5,4},{6,7},{7,6},{8,9},{9,8},{10,11... | collective-permute-start | bytes 49160 | tf_op jit(solution)/shard_map/ppermute | solution.py:299
  48.2 2.2 %collective-permute-done.2 = bf16[16,512]{1,0:T(8,128)(2,1)S(1)} collective-permute-done((bf16[16,512]{1,0:T(8,128)(2,1)S(1)}, bf16[16,512]{1,0:T(8,128)(2,1)S(1)}, u32[]{:S(2)}, u32[]{:S(2)}) %collective-permute-start.2) | collective-permute-done | bytes 16416 | tf_op jit(solution)/shard_map/ppermute | solution.py:299
  50.4 0.6 %fusion = bf16[16,512]{1,0:T(8,128)(2,1)} fusion(bf16[16,512]{1,0:T(8,128)(2,1)S(1)} %collective-permute-done.2, f32[2,16,512]{2,1,0:T(8,128)S(1)} %convert_reduce_fusion, pred[]{:T(512)S(6)} %eq.5), kind=kLoop, calls=%fused_computation.2 | loop fusion | flops 32768 | bytes 98305 | tf_op jit(solution)/shard_map/convert_element_type | solution.py:300
  (2 shorter events, 0.0 us)
Async XLA Ops:
  0.0 8.2 %copy-start = (bf16[16,1024]{1,0:T(8,128)(2,1)S(1)}, bf16[16,1024]{1,0:T(8,128)(2,1)}, u32[]{:S(2)}) copy-start(bf16[16,1024]{1,0:T(8,128)(2,1)} %q_ref.1) | copy-start | bytes 98308
  2.2 24.0 %all-to-all-start = ((bf16[16,272,128]{2,1,0:T(8,128)(2,1)}), bf16[16,272,128]{2,1,0:T(8,128)(2,1)S(1)}, u32[]{:S(2)}, u32[]{:S(2)}) async-start(bf16[16,272,128]{2,1,0:T(8,128)(2,1)} %pack.1), calls=%async_computation | async-start | bytes 2228224 | tf_op jit(solution)/shard_map/all_to_all | solution.py:250
  8.2 13.7 %collective-permute-start = (bf16[16,1024]{1,0:T(8,128)(2,1)S(1)}, bf16[16,1024]{1,0:T(8,128)(2,1)S(1)}, u32[]{:S(2)}, u32[]{:S(2)}) collective-permute-start(bf16[16,1024]{1,0:T(8,128)(2,1)S(1)} %copy-done), channel_id=1, source_target_pairs={{0,128},{8,136},{16,144},{24,152},{32,160},{40,168},{48,176},{56,1... | collective-permute-start | bytes 98312 | tf_op jit(solution)/shard_map/ppermute | solution.py:237
  26.9 5.9 %collective-permute-start.1 = (bf16[144,128]{1,0:T(8,128)(2,1)S(1)}, bf16[144,128]{1,0:T(8,128)(2,1)S(1)}, u32[]{:S(2)}, u32[]{:S(2)}) collective-permute-start(bf16[144,128]{1,0:T(8,128)(2,1)S(1)} %partner.1), channel_id=1, source_target_pairs={{0,128},{8,136},{16,144},{24,152},{32,160},{40,168},{48,176},{56,1... | collective-permute-start | bytes 110600 | tf_op jit(solution)/shard_map/ppermute | solution.py:271
  42.7 7.7 %collective-permute-start.2 = (bf16[16,512]{1,0:T(8,128)(2,1)S(1)}, bf16[16,512]{1,0:T(8,128)(2,1)S(1)}, u32[]{:S(2)}, u32[]{:S(2)}) collective-permute-start(bf16[16,512]{1,0:T(8,128)(2,1)S(1)} %fusion.1), channel_id=1, source_target_pairs={{0,1},{1,0},{2,3},{3,2},{4,5},{5,4},{6,7},{7,6},{8,9},{9,8},{10,11... | collective-permute-start | bytes 49160 | tf_op jit(solution)/shard_map/ppermute | solution.py:299

commit v4 on v3

--- a/solution.py
+++ b/solution.py
@@ -52,11 +52,11 @@
         length[slot] = len_ref[p]
         target[slot] = dest_ref[p]
         places.append((block, other * 2 * width + rank * plen))
-    row = lax.broadcasted_iota(jnp.int32, (16, 128), 0)
-    lane = lax.broadcasted_iota(jnp.int32, (16, 128), 1)
+    row = lax.broadcasted_iota(jnp.int32, (8, 128), 0)
+    lane = lax.broadcasted_iota(jnp.int32, (8, 128), 1)
     pos = lane % plen
     second = (lane // plen) % CAP == 1
-    lower = row < 8
+    lower = row < 4
     for b in range(blocks):
         s = b * 2 * CAP
         limit = jnp.where(
@@ -88,24 +88,24 @@
 
 def prompt_scores(q, got_ref, other, scale):
     blocks, rows, _ = got_ref.shape
-    width = (rows - 16) // 4
+    width = (rows - 8) // 4
     at = other * 2 * width
     seq = lax.broadcasted_iota(jnp.int32, (q.shape[0], 128), 0) // 8
-    left = lax.broadcasted_iota(jnp.int32, (8, 128), 1) < width
+    left = lax.broadcasted_iota(jnp.int32, (1, 128), 1) < width
     out = []
     for b in range(0, blocks, 2):
         keys = jnp.concatenate([got_ref[b, at : at + width, :], got_ref[b + 1, at : at + width, :]], axis=0)
         s = lax.dot_general(q, keys, NT, preferred_element_type=jnp.float32) * scale
         meta0 = got_ref[b, 4 * width :, :].astype(jnp.float32)
         meta1 = got_ref[b + 1, 4 * width :, :].astype(jnp.float32)
-        code = jnp.where(left, meta0[other * 8 : other * 8 + 8], meta1[other * 8 : other * 8 + 8])[0:1]
+        code = jnp.where(left, meta0[other * 4 : other * 4 + 1], meta1[other * 4 : other * 4 + 1])
         out.append(jnp.where(seq == code.astype(jnp.int32), s, NEG))
     return out
 
 
 def prompt_sum(weights, got_ref, other):
     blocks, rows, _ = got_ref.shape
-    width = (rows - 16) // 4
+    width = (rows - 8) // 4
     at = other * 2 * width + width
     total = None
     for i, b in enumerate(range(0, blocks, 2)):
@@ -237,7 +237,7 @@
     far_queries = lax.ppermute(queries, "pool", swap)
     packed = pl.pallas_call(
         functools.partial(pack_kernel, half),
-        out_shape=jax.ShapeDtypeStruct((half, 4 * width + 16, HD), jnp.bfloat16),
+        out_shape=jax.ShapeDtypeStruct((half, 4 * width + 8, HD), jnp.bfloat16),
         in_specs=[anywhere] * 5,
         out_specs=pl.BlockSpec(memory_space=VMEM),
         scratch_shapes=[SMEM((prompts,), jnp.int32)] * 3

time: 52 us -> 51.7 us (level)
  no operation moved by 1% of the time
where the time goes in v4:
time: 51.7 us; the launch traced here: 50.7 us
  starting transfers between devices  17.8 us (34%)
  waiting for transfers between devices  13.3 us (26%)
  Pallas kernels  10.4 us (20%)
  blocking collectives  8.48 us (16%)
  other arithmetic  0.64 us (1%)
    all_to_all x1, blocking collectives, shards(): parts = lax.all_to_all(parts, 'tensor', 0, 0, axis_index_groups=ring)  8.48 us
    ppermute x1, waiting for transfers between devices, shards(): far_queries = lax.ppermute(queries, 'pool', swap)  6.76 us
    all_to_all x1, starting transfers between devices, shards(): got = lax.all_to_all(packed, 'pool', 0, 0, axis_index_groups=halves)  5.94 us
    ppermute x1, starting transfers between devices, shards(): away = lax.ppermute(away, 'tensor', [(i, i ^ 1) for i in range(pieces)])  5.49 us
    all_to_all x1, waiting for transfers between devices, shards(): got = lax.all_to_all(packed, 'pool', 0, 0, axis_index_groups=halves)  4.28 us
    ppermute x1, starting transfers between devices, shards(): far_queries = lax.ppermute(queries, 'pool', swap)  3.36 us
    pallas_call x1, Pallas kernels, shards(): pl.pallas_call(functools.partial(cache_kernel, scale), out_shape=[jax.Sha...  3.24 us
    ppermute x1, starting transfers between devices, shards(): back = lax.ppermute(back, 'pool', swap)  3.05 us
  transfers between devices with their start and end apart: 4, of which 3 were waited for; matrix products, arithmetic and copies ran while one was open for 0% of the time, Pallas kernels for 12%

profile of v4, /device:TPU:6, one launch (start us, length us, event | category | flops | bytes accessed | tf_op | source)
XLA Modules:
  0.0 50.7 jit_solution(16064312421343947859)
XLA Ops:
  0.0 0.0 copy-start
  0.0 2.2 %pack.1 = bf16[16,264,128]{2,1,0:T(8,128)(2,1)} custom-call(s32[32]{0:T(128)} %bitcast.9, s32[32]{0:T(128)} %dest_hbm.1, s32[32]{0:T(128)} %len_hbm.1, bf16[32,32,128]{2,1,0:T(8,128)(2,1)} %keys_hbm.1, bf16[32,32,128]{2,1,0:T(8,128)(2,1)} %values_hbm.1), custom_call_target="tpu_custom_call" | custom-call | tf_op jit(solution)/shard_map/pack/pallas_call | solution.py:238
  2.2 5.9 %all-to-all-start = ((bf16[16,264,128]{2,1,0:T(8,128)(2,1)}), bf16[16,264,128]{2,1,0:T(8,128)(2,1)S(1)}, u32[]{:S(2)}, u32[]{:S(2)}) async-start(bf16[16,264,128]{2,1,0:T(8,128)(2,1)} %pack.1), calls=%async_computation | async-start | bytes 2162688 | tf_op jit(solution)/shard_map/all_to_all | solution.py:250
  8.2 0.0 copy-done
  8.2 3.4 %collective-permute-start = (bf16[16,1024]{1,0:T(8,128)(2,1)S(1)}, bf16[16,1024]{1,0:T(8,128)(2,1)S(1)}, u32[]{:S(2)}, u32[]{:S(2)}) collective-permute-start(bf16[16,1024]{1,0:T(8,128)(2,1)S(1)} %copy-done), channel_id=1, source_target_pairs={{0,128},{8,136},{16,144},{24,152},{32,160},{40,168},{48,176},{56,1... | collective-permute-start | bytes 98312 | tf_op jit(solution)/shard_map/ppermute | solution.py:237
  11.5 3.2 %cache.1 = (f32[128,128]{1,0:T(8,128)S(1)}, f32[128,128]{1,0:T(8,128)S(1)}, f32[128,128]{1,0:T(8,128)S(1)}, f32[128,128]{1,0:T(8,128)S(1)}, bf16[256,4096]{1,0:T(8,128)(2,1)S(1)}) custom-call(s32[16]{0:T(128)} %lens_ref.1, bf16[16,1024]{1,0:T(8,128)(2,1)} %q_ref.1, bf16[16,256,128]{2,1,0:T(8,128)(2,1)} %keys_ref.1, bf16[16,256,128]{2,1,0:T(8,128)(2,1)} %values_ref.1, ...), custom_call_target="tpu_custom_call" | custom-call | flops 200000000 | bytes 12000000 | tf_op jit(solution)/shard_map/cache/pallas_call | solution.py:251
  14.8 6.8 %collective-permute-done.q_ref = bf16[16,1024]{1,0:T(8,128)(2,1)S(1)} collective-permute-done((bf16[16,1024]{1,0:T(8,128)(2,1)S(1)}, bf16[16,1024]{1,0:T(8,128)(2,1)S(1)}, u32[]{:S(2)}, u32[]{:S(2)}) %collective-permute-start) | collective-permute-done | bytes 32800 | tf_op jit(solution)/shard_map/ppermute | solution.py:237
  21.5 4.3 %all-to-all-done.got_ref = bf16[16,264,128]{2,1,0:T(8,128)(2,1)S(1)} async-done(((bf16[16,264,128]{2,1,0:T(8,128)(2,1)}), bf16[16,264,128]{2,1,0:T(8,128)(2,1)S(1)}, u32[]{:S(2)}, u32[]{:S(2)}) %all-to-all-start) | async-done | bytes 1081376 | tf_op jit(solution)/shard_map/all_to_all | solution.py:250
  25.8 0.7 %partner.1 = bf16[144,128]{1,0:T(8,128)(2,1)S(1)} custom-call(bf16[16,1024]{1,0:T(8,128)(2,1)S(1)} %collective-permute-done.q_ref, bf16[16,264,128]{2,1,0:T(8,128)(2,1)S(1)} %all-to-all-done.got_ref), custom_call_target="tpu_custom_call" | custom-call | tf_op jit(solution)/shard_map/partner/pallas_call | solution.py:262
  26.5 3.0 %collective-permute-start.1 = (bf16[144,128]{1,0:T(8,128)(2,1)S(1)}, bf16[144,128]{1,0:T(8,128)(2,1)S(1)}, u32[]{:S(2)}, u32[]{:S(2)}) collective-permute-start(bf16[144,128]{1,0:T(8,128)(2,1)S(1)} %partner.1), channel_id=1, source_target_pairs={{0,128},{8,136},{16,144},{24,152},{32,160},{40,168},{48,176},{56,1... | collective-permute-start | bytes 110600 | tf_op jit(solution)/shard_map/ppermute | solution.py:271
  29.6 2.8 %own.1 = (f32[128,128]{1,0:T(8,128)S(1)}, f32[128,128]{1,0:T(8,128)S(1)}, f32[128,128]{1,0:T(8,128)S(1)}, bf16[768,4096]{1,0:T(8,128)(2,1)S(1)}) custom-call(f32[128,128]{1,0:T(8,128)S(1)} %get-tuple-element.18.q_ref, bf16[16,264,128]{2,1,0:T(8,128)(2,1)S(1)} %all-to-all-done.got_ref, f32[128,128]{1,0:T(8,128)S(1)} %get-tuple-element.20.cache_ref, ...), custom_call_target="tpu_custom_call" | custom-call | flops 100000000 | bytes 2000000 | tf_op jit(solution)/shard_map/own/pallas_call | solution.py:272
  32.4 0.0 collective-permute-done.1.back_ref
  32.4 1.4 %project.1 = bf16[8,16,512]{2,1,0:T(8,128)(2,1)S(1)} custom-call(f32[128,128]{1,0:T(8,128)S(1)} %get-tuple-element.23.main_ref, f32[128,128]{1,0:T(8,128)S(1)} %get-tuple-element.24.top_ref, f32[128,128]{1,0:T(8,128)S(1)} %get-tuple-element.25.sum_ref, bf16[144,128]{1,0:T(8,128)(2,1)S(1)} %collective-permute-done.1.back_ref, ...), custom_call_target="tpu_custom_call" | custom-call | tf_op jit(solution)/shard_map/project/pallas_call | solution.py:282
  33.8 8.5 %all_to_all.10 = bf16[4,2,16,512]{3,2,1,0:T(8,128)(2,1)S(1)} all-to-all(bf16[4,2,16,512]{3,2,1,0:T(8,128)(2,1)S(1)} %bitcast.8), channel_id=1, replica_groups={{0,2,4,6},{1,3,5,7},{8,10,12,14},{9,11,13,15},{16,18,20,22},{17,19,21,2..., dimensions={0} | all-to-all | bytes 262144 | tf_op jit(solution)/shard_map/all_to_all | solution.py:295
  42.3 5.5 %collective-permute-start.2 = (bf16[16,512]{1,0:T(8,128)(2,1)S(1)}, bf16[16,512]{1,0:T(8,128)(2,1)S(1)}, u32[]{:S(2)}, u32[]{:S(2)}) collective-permute-start(bf16[16,512]{1,0:T(8,128)(2,1)S(1)} %fusion.1), channel_id=1, source_target_pairs={{0,1},{1,0},{2,3},{3,2},{4,5},{5,4},{6,7},{7,6},{8,9},{9,8},{10,11... | collective-permute-start | bytes 49160 | tf_op jit(solution)/shard_map/ppermute | solution.py:299
  47.8 2.2 %collective-permute-done.2 = bf16[16,512]{1,0:T(8,128)(2,1)S(1)} collective-permute-done((bf16[16,512]{1,0:T(8,128)(2,1)S(1)}, bf16[16,512]{1,0:T(8,128)(2,1)S(1)}, u32[]{:S(2)}, u32[]{:S(2)}) %collective-permute-start.2) | collective-permute-done | bytes 16416 | tf_op jit(solution)/shard_map/ppermute | solution.py:299
  50.1 0.6 %fusion = bf16[16,512]{1,0:T(8,128)(2,1)} fusion(bf16[16,512]{1,0:T(8,128)(2,1)S(1)} %collective-permute-done.2, f32[2,16,512]{2,1,0:T(8,128)S(1)} %convert_reduce_fusion, pred[]{:T(512)S(6)} %eq.5), kind=kLoop, calls=%fused_computation.2 | loop fusion | flops 32768 | bytes 98305 | tf_op jit(solution)/shard_map/convert_element_type | solution.py:300
  (2 shorter events, 0.0 us)
Async XLA Ops:
  0.0 8.2 %copy-start = (bf16[16,1024]{1,0:T(8,128)(2,1)S(1)}, bf16[16,1024]{1,0:T(8,128)(2,1)}, u32[]{:S(2)}) copy-start(bf16[16,1024]{1,0:T(8,128)(2,1)} %q_ref.1) | copy-start | bytes 98308
  2.2 23.6 %all-to-all-start = ((bf16[16,264,128]{2,1,0:T(8,128)(2,1)}), bf16[16,264,128]{2,1,0:T(8,128)(2,1)S(1)}, u32[]{:S(2)}, u32[]{:S(2)}) async-start(bf16[16,264,128]{2,1,0:T(8,128)(2,1)} %pack.1), calls=%async_computation | async-start | bytes 2162688 | tf_op jit(solution)/shard_map/all_to_all | solution.py:250
  8.2 13.4 %collective-permute-start = (bf16[16,1024]{1,0:T(8,128)(2,1)S(1)}, bf16[16,1024]{1,0:T(8,128)(2,1)S(1)}, u32[]{:S(2)}, u32[]{:S(2)}) collective-permute-start(bf16[16,1024]{1,0:T(8,128)(2,1)S(1)} %copy-done), channel_id=1, source_target_pairs={{0,128},{8,136},{16,144},{24,152},{32,160},{40,168},{48,176},{56,1... | collective-permute-start | bytes 98312 | tf_op jit(solution)/shard_map/ppermute | solution.py:237
  26.5 5.9 %collective-permute-start.1 = (bf16[144,128]{1,0:T(8,128)(2,1)S(1)}, bf16[144,128]{1,0:T(8,128)(2,1)S(1)}, u32[]{:S(2)}, u32[]{:S(2)}) collective-permute-start(bf16[144,128]{1,0:T(8,128)(2,1)S(1)} %partner.1), channel_id=1, source_target_pairs={{0,128},{8,136},{16,144},{24,152},{32,160},{40,168},{48,176},{56,1... | collective-permute-start | bytes 110600 | tf_op jit(solution)/shard_map/ppermute | solution.py:271
  42.3 7.7 %collective-permute-start.2 = (bf16[16,512]{1,0:T(8,128)(2,1)S(1)}, bf16[16,512]{1,0:T(8,128)(2,1)S(1)}, u32[]{:S(2)}, u32[]{:S(2)}) collective-permute-start(bf16[16,512]{1,0:T(8,128)(2,1)S(1)} %fusion.1), channel_id=1, source_target_pairs={{0,1},{1,0},{2,3},{3,2},{4,5},{5,4},{6,7},{7,6},{8,9},{9,8},{10,11... | collective-permute-start | bytes 49160 | tf_op jit(solution)/shard_map/ppermute | solution.py:299

commit v5 on v3

--- a/solution.py
+++ b/solution.py
@@ -10,8 +10,9 @@
 
 HD = 128
 CAP = 2
+GROUP = 4
 EARLY = 256
-LATE = 0
+LATE = 128
 NEG = -(2.0**99)
 VMEM = pltpu.VMEM
 SMEM = pltpu.SMEM
@@ -86,31 +87,35 @@
     return [scratch[pl.ds(s, heads, stride=seqs), :] for s in range(seqs)]
 
 
+def group(ref, b, at, width):
+    return jnp.concatenate([ref[b + i, at : at + width, :] for i in range(GROUP)], axis=0)
+
+
 def prompt_scores(q, got_ref, other, scale):
     blocks, rows, _ = got_ref.shape
     width = (rows - 16) // 4
-    at = other * 2 * width
     seq = lax.broadcasted_iota(jnp.int32, (q.shape[0], 128), 0) // 8
-    left = lax.broadcasted_iota(jnp.int32, (8, 128), 1) < width
+    left = lax.broadcasted_iota(jnp.int32, (1, 128), 1) < width
     out = []
-    for b in range(0, blocks, 2):
-        keys = jnp.concatenate([got_ref[b, at : at + width, :], got_ref[b + 1, at : at + width, :]], axis=0)
+    for b in range(0, blocks, GROUP):
+        keys = group(got_ref, b, other * 2 * width, width)
         s = lax.dot_general(q, keys, NT, preferred_element_type=jnp.float32) * scale
-        meta0 = got_ref[b, 4 * width :, :].astype(jnp.float32)
-        meta1 = got_ref[b + 1, 4 * width :, :].astype(jnp.float32)
-        code = jnp.where(left, meta0[other * 8 : other * 8 + 8], meta1[other * 8 : other * 8 + 8])[0:1]
-        out.append(jnp.where(seq == code.astype(jnp.int32), s, NEG))
+        for i in range(0, GROUP, 2):
+            meta = [got_ref[b + i + k, 4 * width :, :].astype(jnp.float32)[other * 8 : other * 8 + 1] for k in range(2)]
+            code = jnp.where(left, meta[0], meta[1]).astype(jnp.int32)
+            out.append(jnp.where(seq == code, s[:, i * width : (i + 2) * width], NEG))
     return out
 
 
 def prompt_sum(weights, got_ref, other):
     blocks, rows, _ = got_ref.shape
     width = (rows - 16) // 4
-    at = other * 2 * width + width
+    step = GROUP // 2
     total = None
-    for i, b in enumerate(range(0, blocks, 2)):
-        values = jnp.concatenate([got_ref[b, at : at + width, :], got_ref[b + 1, at : at + width, :]], axis=0)
-        part = jnp.dot(weights[i].astype(jnp.bfloat16), values, preferred_element_type=jnp.float32)
+    for i in range(0, len(weights), step):
+        values = group(got_ref, 2 * i, other * 2 * width + width, width)
+        part = jnp.concatenate([w.astype(jnp.bfloat16) for w in weights[i : i + step]], axis=1)
+        part = jnp.dot(part, values, preferred_element_type=jnp.float32)
         total = part if total is None else total + part
     return total
 
@@ -169,7 +174,9 @@
     load.wait()
 
 
-def project_kernel(main_ref, top_ref, sum_ref, back_ref, weight0_ref, weight1_ref, out_ref, scratch):
+def project_kernel(main_ref, top_ref, sum_ref, back_ref, weight0_ref, weight1_ref, weight_hbm, out_ref, scratch, weight2_ref, sem):
+    load = pltpu.make_async_copy(weight_hbm.at[weight_hbm.shape[0] - LATE :], weight2_ref, sem)
+    load.start()
     pieces, seqs, cols = out_ref.shape
     rows = main_ref.shape[0]
     heads = rows // seqs
@@ -187,14 +194,14 @@
     )
     parts = [0.0] * pieces
     at = 0
-    for c in range(pieces):
-        w = weight0_ref[:, c * cols : (c + 1) * cols]
-        parts[c] += jnp.dot(attended[:, at : at + w.shape[0]], w, preferred_element_type=jnp.float32)
-    at += weight0_ref.shape[0]
-    for c in range(pieces):
-        w = weight1_ref[:, c * cols : (c + 1) * cols]
-        parts[c] += jnp.dot(attended[:, at : at + w.shape[0]], w, preferred_element_type=jnp.float32)
-    at += weight1_ref.shape[0]
+    for weight_ref in (weight0_ref, weight1_ref, weight2_ref):
+        if weight_ref is weight2_ref:
+            load.wait()
+        depth = weight_ref.shape[0]
+        for c in range(pieces):
+            weight = weight_ref[:, c * cols : (c + 1) * cols]
+            parts[c] += jnp.dot(attended[:, at : at + depth], weight, preferred_element_type=jnp.float32)
+        at += depth
     for c in range(pieces):
         out_ref[c] = parts[c].astype(out_ref.dtype)
 
@@ -282,12 +289,12 @@
     parts = pl.pallas_call(
         project_kernel,
         out_shape=jax.ShapeDtypeStruct((pieces, seqs, out_cols // pieces), jnp.bfloat16),
-        in_specs=vmem(6),
+        in_specs=vmem(6) + [anywhere],
         out_specs=pl.BlockSpec(memory_space=VMEM),
-        scratch_shapes=[small],
+        scratch_shapes=[small, VMEM((LATE, out_cols), out_weight.dtype), pltpu.SemaphoreType.DMA],
         compiler_params=pltpu.CompilerParams(vmem_limit_bytes=24 << 20),
         name="project",
-    )(main, top, total, back, weight0, weight)
+    )(main, top, total, back, weight0, weight, in_hbm(out_weight))
     second = lax.axis_index("tensor") % 2 == 1
     ring = [[i for i in range(pieces) if i % 2 == k] for k in range(2)]
     parts, second = lax.optimization_barrier((parts, second))

time: 52 us -> 51.8 us (level)
  the two profiles are of different devices: /device:TPU:6 before, /device:TPU:64 now
where the time goes in v5:
time: 51.8 us; the launch traced here: 51.5 us
  waiting for transfers between devices  20 us (39%)
  starting transfers between devices  10.7 us (21%)
  blocking collectives  10.1 us (19%)
  Pallas kernels  9.98 us (19%)
  other arithmetic  0.64 us (1%)
    ppermute x1, waiting for transfers between devices, shards(): far_queries = lax.ppermute(queries, 'pool', swap)  10.5 us
    all_to_all x1, blocking collectives, shards(): parts = lax.all_to_all(parts, 'tensor', 0, 0, axis_index_groups=ring)  10.1 us
    all_to_all x1, starting transfers between devices, shards(): got = lax.all_to_all(packed, 'pool', 0, 0, axis_index_groups=halves)  5.94 us
    ppermute x1, starting transfers between devices, shards(): away = lax.ppermute(away, 'tensor', [(i, i ^ 1) for i in range(pieces)])  4.58 us
    all_to_all x1, waiting for transfers between devices, shards(): got = lax.all_to_all(packed, 'pool', 0, 0, axis_index_groups=halves)  3.87 us
    ppermute x1, waiting for transfers between devices, shards(): away = lax.ppermute(away, 'tensor', [(i, i ^ 1) for i in range(pieces)])  3.33 us
    pallas_call x1, Pallas kernels, shards(): pl.pallas_call(functools.partial(cache_kernel, scale), out_shape=[jax.Sha...  3.25 us
    pallas_call x1, Pallas kernels, shards(): pl.pallas_call(functools.partial(own_kernel, scale), out_shape=[jax.Shape...  2.5 us
  transfers between devices with their start and end apart: 4, of which 4 were waited for; matrix products, arithmetic and copies ran while one was open for 0% of the time, Pallas kernels for 11%

profile of v5, /device:TPU:64, one launch (start us, length us, event | category | flops | bytes accessed | tf_op | source)
XLA Modules:
  0.0 51.5 jit_solution(10075436197144811032)
XLA Ops:
  0.0 0.0 copy-start
  0.0 2.2 %pack.1 = bf16[16,272,128]{2,1,0:T(8,128)(2,1)} custom-call(s32[32]{0:T(128)} %bitcast.9, s32[32]{0:T(128)} %dest_hbm.1, s32[32]{0:T(128)} %len_hbm.1, bf16[32,32,128]{2,1,0:T(8,128)(2,1)} %keys_hbm.1, bf16[32,32,128]{2,1,0:T(8,128)(2,1)} %values_hbm.1), custom_call_target="tpu_custom_call" | custom-call | tf_op jit(solution)/shard_map/pack/pallas_call | solution.py:245
  2.2 5.9 %all-to-all-start = ((bf16[16,272,128]{2,1,0:T(8,128)(2,1)}), bf16[16,272,128]{2,1,0:T(8,128)(2,1)S(1)}, u32[]{:S(2)}, u32[]{:S(2)}) async-start(bf16[16,272,128]{2,1,0:T(8,128)(2,1)} %pack.1), calls=%async_computation | async-start | bytes 2228224 | tf_op jit(solution)/shard_map/all_to_all | solution.py:257
  8.2 0.0 copy-done
  8.2 0.1 collective-permute-start
  8.3 3.2 %cache.1 = (f32[128,128]{1,0:T(8,128)S(1)}, f32[128,128]{1,0:T(8,128)S(1)}, f32[128,128]{1,0:T(8,128)S(1)}, f32[128,128]{1,0:T(8,128)S(1)}, bf16[256,4096]{1,0:T(8,128)(2,1)S(1)}) custom-call(s32[16]{0:T(128)} %lens_ref.1, bf16[16,1024]{1,0:T(8,128)(2,1)} %q_ref.1, bf16[16,256,128]{2,1,0:T(8,128)(2,1)} %keys_ref.1, bf16[16,256,128]{2,1,0:T(8,128)(2,1)} %values_ref.1, ...), custom_call_target="tpu_custom_call" | custom-call | flops 200000000 | bytes 12000000 | tf_op jit(solution)/shard_map/cache/pallas_call | solution.py:258
  11.5 10.5 %collective-permute-done.q_ref = bf16[16,1024]{1,0:T(8,128)(2,1)S(1)} collective-permute-done((bf16[16,1024]{1,0:T(8,128)(2,1)S(1)}, bf16[16,1024]{1,0:T(8,128)(2,1)S(1)}, u32[]{:S(2)}, u32[]{:S(2)}) %collective-permute-start) | collective-permute-done | bytes 32800 | tf_op jit(solution)/shard_map/ppermute | solution.py:244
  22.0 3.9 %all-to-all-done.got_ref = bf16[16,272,128]{2,1,0:T(8,128)(2,1)S(1)} async-done(((bf16[16,272,128]{2,1,0:T(8,128)(2,1)}), bf16[16,272,128]{2,1,0:T(8,128)(2,1)S(1)}, u32[]{:S(2)}, u32[]{:S(2)}) %all-to-all-start) | async-done | bytes 1114144 | tf_op jit(solution)/shard_map/all_to_all | solution.py:257
  25.9 0.5 %partner.1 = bf16[144,128]{1,0:T(8,128)(2,1)S(1)} custom-call(bf16[16,1024]{1,0:T(8,128)(2,1)S(1)} %collective-permute-done.q_ref, bf16[16,272,128]{2,1,0:T(8,128)(2,1)S(1)} %all-to-all-done.got_ref), custom_call_target="tpu_custom_call" | custom-call | tf_op jit(solution)/shard_map/partner/pallas_call | solution.py:269
  26.4 0.1 collective-permute-start.1
  26.5 2.5 %own.1 = (f32[128,128]{1,0:T(8,128)S(1)}, f32[128,128]{1,0:T(8,128)S(1)}, f32[128,128]{1,0:T(8,128)S(1)}, bf16[640,4096]{1,0:T(8,128)(2,1)S(1)}) custom-call(f32[128,128]{1,0:T(8,128)S(1)} %get-tuple-element.18.q_ref, bf16[16,272,128]{2,1,0:T(8,128)(2,1)S(1)} %all-to-all-done.got_ref, f32[128,128]{1,0:T(8,128)S(1)} %get-tuple-element.20.cache_ref, ...), custom_call_target="tpu_custom_call" | custom-call | flops 100000000 | bytes 2000000 | tf_op jit(solution)/shard_map/own/pallas_call | solution.py:279
  29.0 2.3 %collective-permute-done.1.back_ref = bf16[144,128]{1,0:T(8,128)(2,1)S(1)} collective-permute-done((bf16[144,128]{1,0:T(8,128)(2,1)S(1)}, bf16[144,128]{1,0:T(8,128)(2,1)S(1)}, u32[]{:S(2)}, u32[]{:S(2)}) %collective-permute-start.1) | collective-permute-done | bytes 36896 | tf_op jit(solution)/shard_map/ppermute | solution.py:278
  31.4 1.5 %project.1 = bf16[8,16,512]{2,1,0:T(8,128)(2,1)S(1)} custom-call(f32[128,128]{1,0:T(8,128)S(1)} %get-tuple-element.23.main_ref, f32[128,128]{1,0:T(8,128)S(1)} %get-tuple-element.24.top_ref, f32[128,128]{1,0:T(8,128)S(1)} %get-tuple-element.25.sum_ref, bf16[144,128]{1,0:T(8,128)(2,1)S(1)} %collective-permute-done.1.back_ref, ...), custom_call_target="tpu_custom_call" | custom-call | tf_op jit(solution)/shard_map/project/pallas_call | solution.py:289
  32.9 10.1 %all_to_all.10 = bf16[4,2,16,512]{3,2,1,0:T(8,128)(2,1)S(1)} all-to-all(bf16[4,2,16,512]{3,2,1,0:T(8,128)(2,1)S(1)} %bitcast.8), channel_id=1, replica_groups={{0,2,4,6},{1,3,5,7},{8,10,12,14},{9,11,13,15},{16,18,20,22},{17,19,21,2..., dimensions={0} | all-to-all | bytes 262144 | tf_op jit(solution)/shard_map/all_to_all | solution.py:302
  43.0 4.6 %collective-permute-start.2 = (bf16[16,512]{1,0:T(8,128)(2,1)S(1)}, bf16[16,512]{1,0:T(8,128)(2,1)S(1)}, u32[]{:S(2)}, u32[]{:S(2)}) collective-permute-start(bf16[16,512]{1,0:T(8,128)(2,1)S(1)} %fusion.1), channel_id=1, source_target_pairs={{0,1},{1,0},{2,3},{3,2},{4,5},{5,4},{6,7},{7,6},{8,9},{9,8},{10,11... | collective-permute-start | bytes 49160 | tf_op jit(solution)/shard_map/ppermute | solution.py:306
  47.5 3.3 %collective-permute-done.2 = bf16[16,512]{1,0:T(8,128)(2,1)S(1)} collective-permute-done((bf16[16,512]{1,0:T(8,128)(2,1)S(1)}, bf16[16,512]{1,0:T(8,128)(2,1)S(1)}, u32[]{:S(2)}, u32[]{:S(2)}) %collective-permute-start.2) | collective-permute-done | bytes 16416 | tf_op jit(solution)/shard_map/ppermute | solution.py:306
  50.9 0.6 %fusion = bf16[16,512]{1,0:T(8,128)(2,1)} fusion(bf16[16,512]{1,0:T(8,128)(2,1)S(1)} %collective-permute-done.2, f32[2,16,512]{2,1,0:T(8,128)S(1)} %convert_reduce_fusion, pred[]{:T(512)S(6)} %eq.5), kind=kLoop, calls=%fused_computation.2 | loop fusion | flops 32768 | bytes 98305 | tf_op jit(solution)/shard_map/convert_element_type | solution.py:307
  (2 shorter events, 0.0 us)
Async XLA Ops:
  0.0 8.2 %copy-start = (bf16[16,1024]{1,0:T(8,128)(2,1)S(1)}, bf16[16,1024]{1,0:T(8,128)(2,1)}, u32[]{:S(2)}) copy-start(bf16[16,1024]{1,0:T(8,128)(2,1)} %q_ref.1) | copy-start | bytes 98308
  2.2 23.7 %all-to-all-start = ((bf16[16,272,128]{2,1,0:T(8,128)(2,1)}), bf16[16,272,128]{2,1,0:T(8,128)(2,1)S(1)}, u32[]{:S(2)}, u32[]{:S(2)}) async-start(bf16[16,272,128]{2,1,0:T(8,128)(2,1)} %pack.1), calls=%async_computation | async-start | bytes 2228224 | tf_op jit(solution)/shard_map/all_to_all | solution.py:257
  8.2 13.8 %collective-permute-start = (bf16[16,1024]{1,0:T(8,128)(2,1)S(1)}, bf16[16,1024]{1,0:T(8,128)(2,1)S(1)}, u32[]{:S(2)}, u32[]{:S(2)}) collective-permute-start(bf16[16,1024]{1,0:T(8,128)(2,1)S(1)} %copy-done), channel_id=1, source_target_pairs={{0,128},{8,136},{16,144},{24,152},{32,160},{40,168},{48,176},{56,1... | collective-permute-start | bytes 98312 | tf_op jit(solution)/shard_map/ppermute | solution.py:244
  26.4 4.9 %collective-permute-start.1 = (bf16[144,128]{1,0:T(8,128)(2,1)S(1)}, bf16[144,128]{1,0:T(8,128)(2,1)S(1)}, u32[]{:S(2)}, u32[]{:S(2)}) collective-permute-start(bf16[144,128]{1,0:T(8,128)(2,1)S(1)} %partner.1), channel_id=1, source_target_pairs={{0,128},{8,136},{16,144},{24,152},{32,160},{40,168},{48,176},{56,1... | collective-permute-start | bytes 110600 | tf_op jit(solution)/shard_map/ppermute | solution.py:278
  43.0 7.9 %collective-permute-start.2 = (bf16[16,512]{1,0:T(8,128)(2,1)S(1)}, bf16[16,512]{1,0:T(8,128)(2,1)S(1)}, u32[]{:S(2)}, u32[]{:S(2)}) collective-permute-start(bf16[16,512]{1,0:T(8,128)(2,1)S(1)} %fusion.1), channel_id=1, source_target_pairs={{0,1},{1,0},{2,3},{3,2},{4,5},{5,4},{6,7},{7,6},{8,9},{9,8},{10,11... | collective-permute-start | bytes 49160 | tf_op jit(solution)/shard_map/ppermute | solution.py:306

commit v6 on v5

--- a/solution.py
+++ b/solution.py
@@ -12,7 +12,7 @@
 CAP = 2
 GROUP = 4
 EARLY = 256
-LATE = 128
+LATE = 512
 NEG = -(2.0**99)
 VMEM = pltpu.VMEM
 SMEM = pltpu.SMEM
@@ -159,9 +159,11 @@
     load.wait()
 
 
-def own_kernel(scale, q_ref, got_ref, cache_ref, cache_top_ref, cache_sum_ref, weight_hbm, out_ref, top_ref, sum_ref, weight_ref, sem):
+def own_kernel(scale, q_ref, got_ref, cache_ref, cache_top_ref, cache_sum_ref, weight_hbm, out_ref, top_ref, sum_ref, weight_ref, late_ref, sem, sems):
     load = pltpu.make_async_copy(weight_hbm.at[EARLY : weight_hbm.shape[0] - LATE], weight_ref, sem)
     load.start()
+    x = lax.axis_index("tensor") >> 1
+    loads = late_loads([x ^ 1, x ^ 2], weight_hbm, late_ref, sems)
     scores = prompt_scores(q_ref[...].astype(jnp.bfloat16), got_ref, 0, scale)
     top = jnp.max(functools.reduce(jnp.maximum, scores), axis=1, keepdims=True)
     top = jnp.maximum(top, cache_top_ref[...])
@@ -171,13 +173,47 @@
     out_ref[...] = prompt_sum(exps, got_ref, 0) + cache_ref[...] * near
     top_ref[...] = top
     sum_ref[...] = total + cache_sum_ref[...] * near
-    load.wait()
-
-
-def project_kernel(main_ref, top_ref, sum_ref, back_ref, weight0_ref, weight1_ref, weight_hbm, out_ref, scratch, weight2_ref, sem):
-    load = pltpu.make_async_copy(weight_hbm.at[weight_hbm.shape[0] - LATE :], weight2_ref, sem)
-    load.start()
-    pieces, seqs, cols = out_ref.shape
+    for copy in [load] + loads:
+        copy.wait()
+
+
+def late_loads(places, weight_hbm, late_ref, sems):
+    cols = late_ref.shape[2]
+    rows = pl.ds(weight_hbm.shape[0] - LATE, LATE)
+    loads = []
+    for k, place in enumerate(places):
+        at = pl.ds(pl.multiple_of(place * cols, cols), cols)
+        loads.append(pltpu.make_async_copy(weight_hbm.at[rows, at], late_ref.at[k], sems.at[k]))
+        loads[-1].start()
+    return loads
+
+
+def columns(attended, places, weights, late_ref, loads, out_ref):
+    cols = late_ref.shape[2]
+    step = cols // 2
+    parts = []
+    for place in places:
+        for h in range(2):
+            span = pl.ds(pl.multiple_of(place * cols + h * step, step), step)
+            part, at = 0.0, 0
+            for ref in weights:
+                depth = ref.shape[0]
+                part += jnp.dot(attended[:, at : at + depth], ref[:, span], preferred_element_type=jnp.float32)
+                at += depth
+            parts.append(part)
+    for k in range(len(places)):
+        if loads:
+            loads[k].wait()
+        for h in range(2):
+            span = slice(h * step, (h + 1) * step)
+            part = jnp.dot(attended[:, -LATE:], late_ref[k, :, span], preferred_element_type=jnp.float32)
+            out_ref[k, :, span] = (parts[2 * k + h] + part).astype(out_ref.dtype)
+
+
+def send_kernel(main_ref, top_ref, sum_ref, back_ref, weight0_ref, weight1_ref, late_ref, attended_ref, out_ref, scratch):
+    x = lax.axis_index("tensor") >> 1
+    places = [x ^ 1, x ^ 2]
+    seqs = attended_ref.shape[0]
     rows = main_ref.shape[0]
     heads = rows // seqs
     stats = jnp.concatenate([back_ref[rows:, :].astype(jnp.float32)] * (128 // 16), axis=0)
@@ -192,18 +228,15 @@
     attended = jnp.concatenate(
         [scratch[pl.ds(h, seqs, stride=heads), :].astype(jnp.bfloat16) for h in range(heads)], axis=1
     )
-    parts = [0.0] * pieces
-    at = 0
-    for weight_ref in (weight0_ref, weight1_ref, weight2_ref):
-        if weight_ref is weight2_ref:
-            load.wait()
-        depth = weight_ref.shape[0]
-        for c in range(pieces):
-            weight = weight_ref[:, c * cols : (c + 1) * cols]
-            parts[c] += jnp.dot(attended[:, at : at + depth], weight, preferred_element_type=jnp.float32)
-        at += depth
-    for c in range(pieces):
-        out_ref[c] = parts[c].astype(out_ref.dtype)
+    attended_ref[...] = attended
+    columns(attended, places, (weight0_ref, weight1_ref), late_ref, [], out_ref)
+
+
+def keep_kernel(attended_ref, weight0_ref, weight1_ref, weight_hbm, out_ref, late_ref, sems):
+    x = lax.axis_index("tensor") >> 1
+    places = [x, x ^ 3]
+    loads = late_loads(places, weight_hbm, late_ref, sems)
+    columns(attended_ref[...], places, (weight0_ref, weight1_ref), late_ref, loads, out_ref)
 
 
 def vmem(n):
@@ -276,33 +309,50 @@
         name="partner",
     )(far_queries, got)
     back = lax.ppermute(back, "pool", swap)
-    main, top, total, weight = pl.pallas_call(
+    wide = out_cols // pieces * 2
+    main, top, total, weight, late_send = pl.pallas_call(
         functools.partial(own_kernel, scale),
-        out_shape=[jax.ShapeDtypeStruct((rows, HD), jnp.float32)] * 3 + [VMEM((out_weight.shape[0] - EARLY - LATE, out_cols), out_weight.dtype)],
+        out_shape=[jax.ShapeDtypeStruct((rows, HD), jnp.float32)] * 3 + [VMEM((out_weight.shape[0] - EARLY - LATE, out_cols), out_weight.dtype)]
+        + [VMEM((2, LATE, wide), out_weight.dtype)],
         in_specs=vmem(5) + [anywhere],
-        out_specs=vmem(4),
-        scratch_shapes=[pltpu.SemaphoreType.DMA],
+        out_specs=vmem(5),
+        scratch_shapes=[pltpu.SemaphoreType.DMA, pltpu.SemaphoreType.DMA((2,))],
         compiler_params=pltpu.CompilerParams(vmem_limit_bytes=16 << 20),
         cost_estimate=pl.CostEstimate(flops=100_000_000, bytes_accessed=2_000_000, transcendentals=200_000),
         name="own",
     )(heads_first, got, cache, cache_top, cache_sum, in_hbm(out_weight))
-    parts = pl.pallas_call(
-        project_kernel,
-        out_shape=jax.ShapeDtypeStruct((pieces, seqs, out_cols // pieces), jnp.bfloat16),
-        in_specs=vmem(6) + [anywhere],
+    pairs = jax.ShapeDtypeStruct((2, seqs, wide), jnp.bfloat16)
+    late = [VMEM((2, LATE, wide), out_weight.dtype), pltpu.SemaphoreType.DMA((2,))]
+    attended, send = pl.pallas_call(
+        send_kernel,
+        out_shape=[jax.ShapeDtypeStruct((seqs, q_width), jnp.bfloat16), pairs],
+        in_specs=vmem(7),
+        out_specs=vmem(2),
+        scratch_shapes=[small],
+        compiler_params=pltpu.CompilerParams(vmem_limit_bytes=13 << 20),
+        name="send",
+    )(main, top, total, back, weight0, weight, late_send)
+    keep = pl.pallas_call(
+        keep_kernel,
+        out_shape=pairs,
+        in_specs=vmem(3) + [anywhere],
         out_specs=pl.BlockSpec(memory_space=VMEM),
-        scratch_shapes=[small, VMEM((LATE, out_cols), out_weight.dtype), pltpu.SemaphoreType.DMA],
-        compiler_params=pltpu.CompilerParams(vmem_limit_bytes=24 << 20),
-        name="project",
-    )(main, top, total, back, weight0, weight, in_hbm(out_weight))
+        scratch_shapes=late,
+        compiler_params=pltpu.CompilerParams(vmem_limit_bytes=13 << 20),
+        cost_estimate=pl.CostEstimate(flops=8_000_000_000, bytes_accessed=16_000_000, transcendentals=0),
+        name="keep",
+    )(attended, weight0, weight, in_hbm(out_weight))
     second = lax.axis_index("tensor") % 2 == 1
-    ring = [[i for i in range(pieces) if i % 2 == k] for k in range(2)]
-    parts, second = lax.optimization_barrier((parts, second))
-    parts = parts.reshape(pieces // 2, 2, seqs, out_cols // pieces)
-    parts = lax.all_to_all(parts, "tensor", 0, 0, axis_index_groups=ring)
-    parts = jnp.sum(parts.astype(jnp.float32), axis=0)
-    away = jnp.where(second, parts[0], parts[1]).astype(jnp.bfloat16)
-    near = jnp.where(second, parts[1], parts[0])
+    keep, second = lax.optimization_barrier((keep, second))
+
+    def trade(x, partner):
+        return lax.ppermute(x, "tensor", [(2 * i + k, 2 * partner(i) + k) for i in range(pieces // 2) for k in range(2)])
+
+    sums = keep.astype(jnp.float32) + trade(send, lambda i: i ^ 1).astype(jnp.float32)
+    sums = sums[0] + trade(sums[1].astype(jnp.bfloat16), lambda i: 3 - i).astype(jnp.float32)
+    halves = jnp.split(sums, 2, axis=1)
+    away = jnp.where(second, halves[0], halves[1]).astype(jnp.bfloat16)
+    near = jnp.where(second, halves[1], halves[0])
     away = lax.ppermute(away, "tensor", [(i, i ^ 1) for i in range(pieces)])
     return (near + away.astype(jnp.float32)).astype(jnp.bfloat16)
 

time: 51.8 us -> 51.2 us (0.988)
  the two profiles are of different devices: /device:TPU:64 before, /device:TPU:6 now
where the time goes in v6:
time: 51.2 us; the launch traced here: 50.9 us
  starting transfers between devices  19.7 us (38%)
  waiting for transfers between devices  19.3 us (38%)
  Pallas kernels  11.1 us (22%)
  other arithmetic  0.65 us (1%)
    ppermute x1, waiting for transfers between devices, shards(): far_queries = lax.ppermute(queries, 'pool', swap)  7.11 us
    ppermute x2, waiting for transfers between devices, trade(): lax.ppermute(x, 'tensor', [(2 * i + k, 2 * partner(i) + k) for i in range...  6.19 us
    ppermute x1, starting transfers between devices, shards(): away = lax.ppermute(away, 'tensor', [(i, i ^ 1) for i in range(pieces)])  5.99 us
    all_to_all x1, starting transfers between devices, shards(): got = lax.all_to_all(packed, 'pool', 0, 0, axis_index_groups=halves)  5.94 us
    all_to_all x1, waiting for transfers between devices, shards(): got = lax.all_to_all(packed, 'pool', 0, 0, axis_index_groups=halves)  4.28 us
    ppermute x1, starting transfers between devices, shards(): far_queries = lax.ppermute(queries, 'pool', swap)  3.36 us
    pallas_call x1, Pallas kernels, shards(): pl.pallas_call(functools.partial(cache_kernel, scale), out_shape=[jax.Sha...  3.24 us
    ppermute x1, starting transfers between devices, shards(): back = lax.ppermute(back, 'pool', swap)  3.05 us
  transfers between devices with their start and end apart: 6, of which 5 were waited for; matrix products, arithmetic and copies ran while one was open for 0% of the time, Pallas kernels for 15%

profile of v6, /device:TPU:6, one launch (start us, length us, event | category | flops | bytes accessed | tf_op | source)
XLA Modules:
  0.0 50.9 jit_solution(3695445676932180143)
XLA Ops:
  0.0 0.0 copy-start
  0.0 2.2 %pack.1 = bf16[16,272,128]{2,1,0:T(8,128)(2,1)} custom-call(s32[32]{0:T(128)} %bitcast.7, s32[32]{0:T(128)} %dest_hbm.1, s32[32]{0:T(128)} %len_hbm.1, bf16[32,32,128]{2,1,0:T(8,128)(2,1)} %keys_hbm.1, bf16[32,32,128]{2,1,0:T(8,128)(2,1)} %values_hbm.1), custom_call_target="tpu_custom_call" | custom-call | tf_op jit(solution)/shard_map/pack/pallas_call | solution.py:278
  2.2 5.9 %all-to-all-start = ((bf16[16,272,128]{2,1,0:T(8,128)(2,1)}), bf16[16,272,128]{2,1,0:T(8,128)(2,1)S(1)}, u32[]{:S(2)}, u32[]{:S(2)}) async-start(bf16[16,272,128]{2,1,0:T(8,128)(2,1)} %pack.1), calls=%async_computation | async-start | bytes 2228224 | tf_op jit(solution)/shard_map/all_to_all | solution.py:290
  8.2 0.0 copy-done
  8.2 3.4 %collective-permute-start = (bf16[16,1024]{1,0:T(8,128)(2,1)S(1)}, bf16[16,1024]{1,0:T(8,128)(2,1)S(1)}, u32[]{:S(2)}, u32[]{:S(2)}) collective-permute-start(bf16[16,1024]{1,0:T(8,128)(2,1)S(1)} %copy-done), channel_id=1, source_target_pairs={{0,128},{8,136},{16,144},{24,152},{32,160},{40,168},{48,176},{56,1... | collective-permute-start | bytes 98312 | tf_op jit(solution)/shard_map/ppermute | solution.py:277
  11.6 3.2 %cache.1 = (f32[128,128]{1,0:T(8,128)S(1)}, f32[128,128]{1,0:T(8,128)S(1)}, f32[128,128]{1,0:T(8,128)S(1)}, f32[128,128]{1,0:T(8,128)S(1)}, bf16[256,4096]{1,0:T(8,128)(2,1)S(1)}) custom-call(s32[16]{0:T(128)} %lens_ref.1, bf16[16,1024]{1,0:T(8,128)(2,1)} %q_ref.1, bf16[16,256,128]{2,1,0:T(8,128)(2,1)} %keys_ref.1, bf16[16,256,128]{2,1,0:T(8,128)(2,1)} %values_ref.1, ...), custom_call_target="tpu_custom_call" | custom-call | flops 200000000 | bytes 12000000 | tf_op jit(solution)/shard_map/cache/pallas_call | solution.py:291
  14.8 7.1 %collective-permute-done.q_ref = bf16[16,1024]{1,0:T(8,128)(2,1)S(1)} collective-permute-done((bf16[16,1024]{1,0:T(8,128)(2,1)S(1)}, bf16[16,1024]{1,0:T(8,128)(2,1)S(1)}, u32[]{:S(2)}, u32[]{:S(2)}) %collective-permute-start) | collective-permute-done | bytes 32800 | tf_op jit(solution)/shard_map/ppermute | solution.py:277
  21.9 4.3 %all-to-all-done.got_ref = bf16[16,272,128]{2,1,0:T(8,128)(2,1)S(1)} async-done(((bf16[16,272,128]{2,1,0:T(8,128)(2,1)}), bf16[16,272,128]{2,1,0:T(8,128)(2,1)S(1)}, u32[]{:S(2)}, u32[]{:S(2)}) %all-to-all-start) | async-done | bytes 1114144 | tf_op jit(solution)/shard_map/all_to_all | solution.py:290
  26.2 0.5 %partner.1 = bf16[144,128]{1,0:T(8,128)(2,1)S(1)} custom-call(bf16[16,1024]{1,0:T(8,128)(2,1)S(1)} %collective-permute-done.q_ref, bf16[16,272,128]{2,1,0:T(8,128)(2,1)S(1)} %all-to-all-done.got_ref), custom_call_target="tpu_custom_call" | custom-call | tf_op jit(solution)/shard_map/partner/pallas_call | solution.py:302
  26.7 3.1 %collective-permute-start.1 = (bf16[144,128]{1,0:T(8,128)(2,1)S(1)}, bf16[144,128]{1,0:T(8,128)(2,1)S(1)}, u32[]{:S(2)}, u32[]{:S(2)}) collective-permute-start(bf16[144,128]{1,0:T(8,128)(2,1)S(1)} %partner.1), channel_id=1, source_target_pairs={{0,128},{8,136},{16,144},{24,152},{32,160},{40,168},{48,176},{56,1... | collective-permute-start | bytes 110600 | tf_op jit(solution)/shard_map/ppermute | solution.py:311
  29.8 2.3 %own.1 = (f32[128,128]{1,0:T(8,128)S(1)}, f32[128,128]{1,0:T(8,128)S(1)}, f32[128,128]{1,0:T(8,128)S(1)}, bf16[256,4096]{1,0:T(8,128)(2,1)S(1)}, bf16[2,512,1024]{2,1,0:T(8,128)(2,1)S(1)}) custom-call(f32[128,128]{1,0:T(8,128)S(1)} %get-tuple-element.21.q_ref, bf16[16,272,128]{2,1,0:T(8,128)(2,1)S(1)} %all-to-all-done.got_ref, ...), custom_call_target="tpu_custom_call" | custom-call | flops 100000000 | bytes 2000000 | tf_op jit(solution)/shard_map/own/pallas_call | solution.py:313
  32.1 0.0 collective-permute-done.1.back_ref
  32.1 0.9 %send.1 = (bf16[16,1024]{1,0:T(8,128)(2,1)S(1)}, bf16[2,16,1024]{2,1,0:T(8,128)(2,1)S(1)}) custom-call(f32[128,128]{1,0:T(8,128)S(1)} %get-tuple-element.26.main_ref, f32[128,128]{1,0:T(8,128)S(1)} %get-tuple-element.27.top_ref, f32[128,128]{1,0:T(8,128)S(1)} %get-tuple-element.28.sum_ref, bf16[144,128]{1,0:T(8,128)(2,1)S(1)} %collective-permute-done.1.back_ref, ...), custom_call_target="tpu_custom_call" | custom-call | tf_op jit(solution)/shard_map/send/pallas_call | solution.py:326
  33.0 0.8 %collective-permute-start.2 = (bf16[2,16,1024]{2,1,0:T(8,128)(2,1)S(1)}, bf16[2,16,1024]{2,1,0:T(8,128)(2,1)S(1)}, u32[]{:S(2)}, u32[]{:S(2)}) collective-permute-start(bf16[2,16,1024]{2,1,0:T(8,128)(2,1)S(1)} %get-tuple-element.36), channel_id=1, source_target_pairs={{0,2},{1,3},{2,0},{3,1},{4,6},{5,7},{6,4},{7,5},{8,10},{9,11},{10,... | collective-permute-start | bytes 196616 | tf_op jit(solution)/shard_map/ppermute | solution.py:349
  33.8 1.9 %keep.1 = bf16[2,16,1024]{2,1,0:T(8,128)(2,1)S(1)} custom-call(bf16[16,1024]{1,0:T(8,128)(2,1)S(1)} %get-tuple-element.33.attended_ref, bf16[256,4096]{1,0:T(8,128)(2,1)S(1)} %get-tuple-element.30.weight0_ref, bf16[256,4096]{1,0:T(8,128)(2,1)S(1)} %get-tuple-element.31.weight1_ref, bf16[1024,4096]{1,0:T(8,128)(2,1)} %weight_hbm.5), custom_call_target="tpu_custom_call" | custom-call | flops 8000000000 | bytes 16000000 | tf_op jit(solution)/shard_map/keep/pallas_call | solution.py:335
  35.7 1.5 %collective-permute-done.2 = bf16[2,16,1024]{2,1,0:T(8,128)(2,1)S(1)} collective-permute-done((bf16[2,16,1024]{2,1,0:T(8,128)(2,1)S(1)}, bf16[2,16,1024]{2,1,0:T(8,128)(2,1)S(1)}, u32[]{:S(2)}, u32[]{:S(2)}) %collective-permute-start.2) | collective-permute-done | bytes 65568 | tf_op jit(solution)/shard_map/ppermute | solution.py:349
  37.3 0.6 %collective-permute-start.3 = (bf16[16,1024]{1,0:T(8,128)(2,1)S(1)}, bf16[16,1024]{1,0:T(8,128)(2,1)S(1)}, u32[]{:S(2)}, u32[]{:S(2)}) collective-permute-start(bf16[16,1024]{1,0:T(8,128)(2,1)S(1)} %fusion.1), channel_id=1, source_target_pairs={{0,6},{1,7},{2,4},{3,5},{4,2},{5,3},{6,0},{7,1},{8,14},{9,15},{10,... | collective-permute-start | bytes 98312 | tf_op jit(solution)/shard_map/ppermute | solution.py:349
  37.9 4.6 %collective-permute-done.3 = bf16[16,1024]{1,0:T(8,128)(2,1)S(1)} collective-permute-done((bf16[16,1024]{1,0:T(8,128)(2,1)S(1)}, bf16[16,1024]{1,0:T(8,128)(2,1)S(1)}, u32[]{:S(2)}, u32[]{:S(2)}) %collective-permute-start.3) | collective-permute-done | bytes 32800 | tf_op jit(solution)/shard_map/ppermute | solution.py:349
  42.5 6.0 %collective-permute-start.4 = (bf16[16,512]{1,0:T(8,128)(2,1)S(1)}, bf16[16,512]{1,0:T(8,128)(2,1)S(1)}, u32[]{:S(2)}, u32[]{:S(2)}) collective-permute-start(bf16[16,512]{1,0:T(8,128)(2,1)S(1)} %select_convert_fusion), channel_id=1, source_target_pairs={{0,1},{1,0},{2,3},{3,2},{4,5},{5,4},{6,7},{7,6},{8,9},{9,8},{10,11... | collective-permute-start | bytes 49160 | tf_op jit(solution)/shard_map/ppermute | solution.py:356
  48.5 1.7 %collective-permute-done.4 = bf16[16,512]{1,0:T(8,128)(2,1)S(1)} collective-permute-done((bf16[16,512]{1,0:T(8,128)(2,1)S(1)}, bf16[16,512]{1,0:T(8,128)(2,1)S(1)}, u32[]{:S(2)}, u32[]{:S(2)}) %collective-permute-start.4) | collective-permute-done | bytes 16416 | tf_op jit(solution)/shard_map/ppermute | solution.py:356
  50.3 0.6 %add_convert_fusion = bf16[16,512]{1,0:T(8,128)(2,1)} fusion(bf16[16,512]{1,0:T(8,128)(2,1)S(1)} %collective-permute-done.4, f32[16,1024]{1,0:T(8,128)S(1)} %fusion, pred[]{:T(512)S(6)} %eq.5), kind=kLoop, calls=%fused_computation.5 | loop fusion | flops 32768 | bytes 98305 | tf_op jit(solution)/shard_map/convert_element_type | solution.py:357
  (4 shorter events, 0.0 us)
Async XLA Ops:
  0.0 8.2 %copy-start = (bf16[16,1024]{1,0:T(8,128)(2,1)S(1)}, bf16[16,1024]{1,0:T(8,128)(2,1)}, u32[]{:S(2)}) copy-start(bf16[16,1024]{1,0:T(8,128)(2,1)} %q_ref.1) | copy-start | bytes 98308
  2.2 24.0 %all-to-all-start = ((bf16[16,272,128]{2,1,0:T(8,128)(2,1)}), bf16[16,272,128]{2,1,0:T(8,128)(2,1)S(1)}, u32[]{:S(2)}, u32[]{:S(2)}) async-start(bf16[16,272,128]{2,1,0:T(8,128)(2,1)} %pack.1), calls=%async_computation | async-start | bytes 2228224 | tf_op jit(solution)/shard_map/all_to_all | solution.py:290
  8.2 13.7 %collective-permute-start = (bf16[16,1024]{1,0:T(8,128)(2,1)S(1)}, bf16[16,1024]{1,0:T(8,128)(2,1)S(1)}, u32[]{:S(2)}, u32[]{:S(2)}) collective-permute-start(bf16[16,1024]{1,0:T(8,128)(2,1)S(1)} %copy-done), channel_id=1, source_target_pairs={{0,128},{8,136},{16,144},{24,152},{32,160},{40,168},{48,176},{56,1... | collective-permute-start | bytes 98312 | tf_op jit(solution)/shard_map/ppermute | solution.py:277
  26.7 5.4 %collective-permute-start.1 = (bf16[144,128]{1,0:T(8,128)(2,1)S(1)}, bf16[144,128]{1,0:T(8,128)(2,1)S(1)}, u32[]{:S(2)}, u32[]{:S(2)}) collective-permute-start(bf16[144,128]{1,0:T(8,128)(2,1)S(1)} %partner.1), channel_id=1, source_target_pairs={{0,128},{8,136},{16,144},{24,152},{32,160},{40,168},{48,176},{56,1... | collective-permute-start | bytes 110600 | tf_op jit(solution)/shard_map/ppermute | solution.py:311
  33.0 4.3 %collective-permute-start.2 = (bf16[2,16,1024]{2,1,0:T(8,128)(2,1)S(1)}, bf16[2,16,1024]{2,1,0:T(8,128)(2,1)S(1)}, u32[]{:S(2)}, u32[]{:S(2)}) collective-permute-start(bf16[2,16,1024]{2,1,0:T(8,128)(2,1)S(1)} %get-tuple-element.36), channel_id=1, source_target_pairs={{0,2},{1,3},{2,0},{3,1},{4,6},{5,7},{6,4},{7,5},{8,10},{9,11},{10,... | collective-permute-start | bytes 196616 | tf_op jit(solution)/shard_map/ppermute | solution.py:349
  37.3 5.2 %collective-permute-start.3 = (bf16[16,1024]{1,0:T(8,128)(2,1)S(1)}, bf16[16,1024]{1,0:T(8,128)(2,1)S(1)}, u32[]{:S(2)}, u32[]{:S(2)}) collective-permute-start(bf16[16,1024]{1,0:T(8,128)(2,1)S(1)} %fusion.1), channel_id=1, source_target_pairs={{0,6},{1,7},{2,4},{3,5},{4,2},{5,3},{6,0},{7,1},{8,14},{9,15},{10,... | collective-permute-start | bytes 98312 | tf_op jit(solution)/shard_map/ppermute | solution.py:349
  42.5 7.7 %collective-permute-start.4 = (bf16[16,512]{1,0:T(8,128)(2,1)S(1)}, bf16[16,512]{1,0:T(8,128)(2,1)S(1)}, u32[]{:S(2)}, u32[]{:S(2)}) collective-permute-start(bf16[16,512]{1,0:T(8,128)(2,1)S(1)} %select_convert_fusion), channel_id=1, source_target_pairs={{0,1},{1,0},{2,3},{3,2},{4,5},{5,4},{6,7},{7,6},{8,9},{9,8},{10,11... | collective-permute-start | bytes 49160 | tf_op jit(solution)/shard_map/ppermute | solution.py:356

commit v7 on v6

--- a/solution.py
+++ b/solution.py
@@ -348,8 +348,11 @@
     def trade(x, partner):
         return lax.ppermute(x, "tensor", [(2 * i + k, 2 * partner(i) + k) for i in range(pieces // 2) for k in range(2)])
 
-    sums = keep.astype(jnp.float32) + trade(send, lambda i: i ^ 1).astype(jnp.float32)
-    sums = sums[0] + trade(sums[1].astype(jnp.bfloat16), lambda i: 3 - i).astype(jnp.float32)
+    first = trade(send[1], lambda i: i ^ 1)
+    later = trade(send[0], lambda i: i ^ 1)
+    mirror = (keep[1].astype(jnp.float32) + first.astype(jnp.float32)).astype(jnp.bfloat16)
+    mirror = trade(mirror, lambda i: 3 - i)
+    sums = keep[0].astype(jnp.float32) + later.astype(jnp.float32) + mirror.astype(jnp.float32)
     halves = jnp.split(sums, 2, axis=1)
     away = jnp.where(second, halves[0], halves[1]).astype(jnp.bfloat16)
     near = jnp.where(second, halves[1], halves[0])

time: 51.2 us -> 51.2 us (level)
  starting transfers between devices: 19.7 us -> 21.3 us
  waiting for transfers between devices: 19.3 us -> 17.8 us
    ppermute x2 -> x3, waiting for transfers between devices: 6.19 us -> 4.65 us  [trade(): lax.ppermute(x, 'tensor', [(2 * i + k, 2 * partner(i) + k) for i in range...]
    ppermute x2 -> x3, starting transfers between devices: 1.4 us -> 2.76 us  [trade(): lax.ppermute(x, 'tensor', [(2 * i + k, 2 * partner(i) + k) for i in range...]
  transfers between devices with their start and end apart: 6 -> 7, of which waited for: 5 -> 5; matrix products, arithmetic and copies ran while one was open for 0% -> 0% of each run, Pallas kernels for 15% -> 15%
where the time goes in v7:
time: 51.2 us; the launch traced here: 50.9 us
  starting transfers between devices  21.3 us (42%)
  waiting for transfers between devices  17.8 us (35%)
  Pallas kernels  11.1 us (22%)
  other arithmetic  0.65 us (1%)
    ppermute x1, waiting for transfers between devices, shards(): far_queries = lax.ppermute(queries, 'pool', swap)  7.11 us
    ppermute x1, starting transfers between devices, shards(): away = lax.ppermute(away, 'tensor', [(i, i ^ 1) for i in range(pieces)])  6.21 us
    all_to_all x1, starting transfers between devices, shards(): got = lax.all_to_all(packed, 'pool', 0, 0, axis_index_groups=halves)  5.94 us
    ppermute x3, waiting for transfers between devices, trade(): lax.ppermute(x, 'tensor', [(2 * i + k, 2 * partner(i) + k) for i in range...  4.65 us
    all_to_all x1, waiting for transfers between devices, shards(): got = lax.all_to_all(packed, 'pool', 0, 0, axis_index_groups=halves)  4.28 us
    ppermute x1, starting transfers between devices, shards(): far_queries = lax.ppermute(queries, 'pool', swap)  3.36 us
    pallas_call x1, Pallas kernels, shards(): pl.pallas_call(functools.partial(cache_kernel, scale), out_shape=[jax.Sha...  3.24 us
    ppermute x1, starting transfers between devices, shards(): back = lax.ppermute(back, 'pool', swap)  3.05 us
  transfers between devices with their start and end apart: 7, of which 5 were waited for; matrix products, arithmetic and copies ran while one was open for 0% of the time, Pallas kernels for 15%

profile of v7, /device:TPU:6, one launch (start us, length us, event | category | flops | bytes accessed | tf_op | source)
XLA Modules:
  0.0 50.9 jit_solution(3294825666502939429)
XLA Ops:
  0.0 0.0 copy-start
  0.0 2.2 %pack.1 = bf16[16,272,128]{2,1,0:T(8,128)(2,1)} custom-call(s32[32]{0:T(128)} %bitcast.11, s32[32]{0:T(128)} %dest_hbm.1, s32[32]{0:T(128)} %len_hbm.1, bf16[32,32,128]{2,1,0:T(8,128)(2,1)} %keys_hbm.1, bf16[32,32,128]{2,1,0:T(8,128)(2,1)} %values_hbm.1), custom_call_target="tpu_custom_call" | custom-call | tf_op jit(solution)/shard_map/pack/pallas_call | solution.py:278
  2.2 5.9 %all-to-all-start = ((bf16[16,272,128]{2,1,0:T(8,128)(2,1)}), bf16[16,272,128]{2,1,0:T(8,128)(2,1)S(1)}, u32[]{:S(2)}, u32[]{:S(2)}) async-start(bf16[16,272,128]{2,1,0:T(8,128)(2,1)} %pack.1), calls=%async_computation | async-start | bytes 2228224 | tf_op jit(solution)/shard_map/all_to_all | solution.py:290
  8.2 0.0 copy-done
  8.2 3.4 %collective-permute-start = (bf16[16,1024]{1,0:T(8,128)(2,1)S(1)}, bf16[16,1024]{1,0:T(8,128)(2,1)S(1)}, u32[]{:S(2)}, u32[]{:S(2)}) collective-permute-start(bf16[16,1024]{1,0:T(8,128)(2,1)S(1)} %copy-done), channel_id=1, source_target_pairs={{0,128},{8,136},{16,144},{24,152},{32,160},{40,168},{48,176},{56,1... | collective-permute-start | bytes 98312 | tf_op jit(solution)/shard_map/ppermute | solution.py:277
  11.5 3.2 %cache.1 = (f32[128,128]{1,0:T(8,128)S(1)}, f32[128,128]{1,0:T(8,128)S(1)}, f32[128,128]{1,0:T(8,128)S(1)}, f32[128,128]{1,0:T(8,128)S(1)}, bf16[256,4096]{1,0:T(8,128)(2,1)S(1)}) custom-call(s32[16]{0:T(128)} %lens_ref.1, bf16[16,1024]{1,0:T(8,128)(2,1)} %q_ref.1, bf16[16,256,128]{2,1,0:T(8,128)(2,1)} %keys_ref.1, bf16[16,256,128]{2,1,0:T(8,128)(2,1)} %values_ref.1, ...), custom_call_target="tpu_custom_call" | custom-call | flops 200000000 | bytes 12000000 | tf_op jit(solution)/shard_map/cache/pallas_call | solution.py:291
  14.8 7.1 %collective-permute-done.q_ref = bf16[16,1024]{1,0:T(8,128)(2,1)S(1)} collective-permute-done((bf16[16,1024]{1,0:T(8,128)(2,1)S(1)}, bf16[16,1024]{1,0:T(8,128)(2,1)S(1)}, u32[]{:S(2)}, u32[]{:S(2)}) %collective-permute-start) | collective-permute-done | bytes 32800 | tf_op jit(solution)/shard_map/ppermute | solution.py:277
  21.9 4.3 %all-to-all-done.got_ref = bf16[16,272,128]{2,1,0:T(8,128)(2,1)S(1)} async-done(((bf16[16,272,128]{2,1,0:T(8,128)(2,1)}), bf16[16,272,128]{2,1,0:T(8,128)(2,1)S(1)}, u32[]{:S(2)}, u32[]{:S(2)}) %all-to-all-start) | async-done | bytes 1114144 | tf_op jit(solution)/shard_map/all_to_all | solution.py:290
  26.2 0.5 %partner.1 = bf16[144,128]{1,0:T(8,128)(2,1)S(1)} custom-call(bf16[16,1024]{1,0:T(8,128)(2,1)S(1)} %collective-permute-done.q_ref, bf16[16,272,128]{2,1,0:T(8,128)(2,1)S(1)} %all-to-all-done.got_ref), custom_call_target="tpu_custom_call" | custom-call | tf_op jit(solution)/shard_map/partner/pallas_call | solution.py:302
  26.7 3.1 %collective-permute-start.1 = (bf16[144,128]{1,0:T(8,128)(2,1)S(1)}, bf16[144,128]{1,0:T(8,128)(2,1)S(1)}, u32[]{:S(2)}, u32[]{:S(2)}) collective-permute-start(bf16[144,128]{1,0:T(8,128)(2,1)S(1)} %partner.1), channel_id=1, source_target_pairs={{0,128},{8,136},{16,144},{24,152},{32,160},{40,168},{48,176},{56,1... | collective-permute-start | bytes 110600 | tf_op jit(solution)/shard_map/ppermute | solution.py:311
  29.8 2.3 %own.1 = (f32[128,128]{1,0:T(8,128)S(1)}, f32[128,128]{1,0:T(8,128)S(1)}, f32[128,128]{1,0:T(8,128)S(1)}, bf16[256,4096]{1,0:T(8,128)(2,1)S(1)}, bf16[2,512,1024]{2,1,0:T(8,128)(2,1)S(1)}) custom-call(f32[128,128]{1,0:T(8,128)S(1)} %get-tuple-element.21.q_ref, bf16[16,272,128]{2,1,0:T(8,128)(2,1)S(1)} %all-to-all-done.got_ref, ...), custom_call_target="tpu_custom_call" | custom-call | flops 100000000 | bytes 2000000 | tf_op jit(solution)/shard_map/own/pallas_call | solution.py:313
  32.1 0.0 collective-permute-done.1.back_ref
  32.1 0.9 %send.1 = (bf16[16,1024]{1,0:T(8,128)(2,1)S(1)}, bf16[2,16,1024]{2,1,0:T(8,128)(2,1)S(1)}) custom-call(f32[128,128]{1,0:T(8,128)S(1)} %get-tuple-element.26.main_ref, f32[128,128]{1,0:T(8,128)S(1)} %get-tuple-element.27.top_ref, f32[128,128]{1,0:T(8,128)S(1)} %get-tuple-element.28.sum_ref, bf16[144,128]{1,0:T(8,128)(2,1)S(1)} %collective-permute-done.1.back_ref, ...), custom_call_target="tpu_custom_call" | custom-call | tf_op jit(solution)/shard_map/send/pallas_call | solution.py:326
  33.0 0.9 %collective-permute-start.3 = (bf16[16,1024]{1,0:T(8,128)(2,1)S(1)}, bf16[16,1024]{1,0:T(8,128)(2,1)S(1)}, u32[]{:S(2)}, u32[]{:S(2)}) collective-permute-start(bf16[16,1024]{1,0:T(8,128)(2,1)S(1)} %get-tuple-element.38), channel_id=1, source_target_pairs={{0,2},{1,3},{2,0},{3,1},{4,6},{5,7},{6,4},{7,5},{8,10},{9,11},{10,... | collective-permute-start | bytes 98312 | tf_op jit(solution)/shard_map/ppermute | solution.py:349
  33.9 1.9 %keep.1 = bf16[2,16,1024]{2,1,0:T(8,128)(2,1)S(1)} custom-call(bf16[16,1024]{1,0:T(8,128)(2,1)S(1)} %get-tuple-element.33.attended_ref, bf16[256,4096]{1,0:T(8,128)(2,1)S(1)} %get-tuple-element.30.weight0_ref, bf16[256,4096]{1,0:T(8,128)(2,1)S(1)} %get-tuple-element.31.weight1_ref, bf16[1024,4096]{1,0:T(8,128)(2,1)} %weight_hbm.5), custom_call_target="tpu_custom_call" | custom-call | flops 8000000000 | bytes 16000000 | tf_op jit(solution)/shard_map/keep/pallas_call | solution.py:335
  35.8 1.3 %collective-permute-start.2 = (bf16[16,1024]{1,0:T(8,128)(2,1)S(1)}, bf16[16,1024]{1,0:T(8,128)(2,1)S(1)}, u32[]{:S(2)}, u32[]{:S(2)}) collective-permute-start(bf16[16,1024]{1,0:T(8,128)(2,1)S(1)} %get-tuple-element.37), channel_id=1, source_target_pairs={{0,2},{1,3},{2,0},{3,1},{4,6},{5,7},{6,4},{7,5},{8,10},{9,11},{10,... | collective-permute-start | bytes 98312 | tf_op jit(solution)/shard_map/ppermute | solution.py:349
  37.1 0.0 collective-permute-done.3
  37.1 0.6 %collective-permute-start.4 = (bf16[16,1024]{1,0:T(8,128)(2,1)S(1)}, bf16[16,1024]{1,0:T(8,128)(2,1)S(1)}, u32[]{:S(2)}, u32[]{:S(2)}) collective-permute-start(bf16[16,1024]{1,0:T(8,128)(2,1)S(1)} %fusion), channel_id=1, source_target_pairs={{0,6},{1,7},{2,4},{3,5},{4,2},{5,3},{6,0},{7,1},{8,14},{9,15},{10,... | collective-permute-start | bytes 98312 | tf_op jit(solution)/shard_map/ppermute | solution.py:349
  37.7 2.1 %collective-permute-done.2 = bf16[16,1024]{1,0:T(8,128)(2,1)S(1)} collective-permute-done((bf16[16,1024]{1,0:T(8,128)(2,1)S(1)}, bf16[16,1024]{1,0:T(8,128)(2,1)S(1)}, u32[]{:S(2)}, u32[]{:S(2)}) %collective-permute-start.2) | collective-permute-done | bytes 32800 | tf_op jit(solution)/shard_map/ppermute | solution.py:349
  39.8 2.5 %collective-permute-done.4 = bf16[16,1024]{1,0:T(8,128)(2,1)S(1)} collective-permute-done((bf16[16,1024]{1,0:T(8,128)(2,1)S(1)}, bf16[16,1024]{1,0:T(8,128)(2,1)S(1)}, u32[]{:S(2)}, u32[]{:S(2)}) %collective-permute-start.4) | collective-permute-done | bytes 32800 | tf_op jit(solution)/shard_map/ppermute | solution.py:349
  42.4 6.2 %collective-permute-start.5 = (bf16[16,512]{1,0:T(8,128)(2,1)S(1)}, bf16[16,512]{1,0:T(8,128)(2,1)S(1)}, u32[]{:S(2)}, u32[]{:S(2)}) collective-permute-start(bf16[16,512]{1,0:T(8,128)(2,1)S(1)} %select_convert_fusion), channel_id=1, source_target_pairs={{0,1},{1,0},{2,3},{3,2},{4,5},{5,4},{6,7},{7,6},{8,9},{9,8},{10,11... | collective-permute-start | bytes 49160 | tf_op jit(solution)/shard_map/ppermute | solution.py:359
  48.6 1.7 %collective-permute-done.5 = bf16[16,512]{1,0:T(8,128)(2,1)S(1)} collective-permute-done((bf16[16,512]{1,0:T(8,128)(2,1)S(1)}, bf16[16,512]{1,0:T(8,128)(2,1)S(1)}, u32[]{:S(2)}, u32[]{:S(2)}) %collective-permute-start.5) | collective-permute-done | bytes 16416 | tf_op jit(solution)/shard_map/ppermute | solution.py:359
  50.3 0.6 %add_convert_fusion = bf16[16,512]{1,0:T(8,128)(2,1)} fusion(bf16[16,512]{1,0:T(8,128)(2,1)S(1)} %collective-permute-done.5, f32[16,1024]{1,0:T(8,128)S(1)} %fusion.1, pred[]{:T(512)S(6)} %eq.5), kind=kLoop, calls=%fused_computation.4 | loop fusion | flops 32768 | bytes 98305 | tf_op jit(solution)/shard_map/convert_element_type | solution.py:360
  (4 shorter events, 0.0 us)
Async XLA Ops:
  0.0 8.2 %copy-start = (bf16[16,1024]{1,0:T(8,128)(2,1)S(1)}, bf16[16,1024]{1,0:T(8,128)(2,1)}, u32[]{:S(2)}) copy-start(bf16[16,1024]{1,0:T(8,128)(2,1)} %q_ref.1) | copy-start | bytes 98308
  2.2 24.0 %all-to-all-start = ((bf16[16,272,128]{2,1,0:T(8,128)(2,1)}), bf16[16,272,128]{2,1,0:T(8,128)(2,1)S(1)}, u32[]{:S(2)}, u32[]{:S(2)}) async-start(bf16[16,272,128]{2,1,0:T(8,128)(2,1)} %pack.1), calls=%async_computation | async-start | bytes 2228224 | tf_op jit(solution)/shard_map/all_to_all | solution.py:290
  8.2 13.7 %collective-permute-start = (bf16[16,1024]{1,0:T(8,128)(2,1)S(1)}, bf16[16,1024]{1,0:T(8,128)(2,1)S(1)}, u32[]{:S(2)}, u32[]{:S(2)}) collective-permute-start(bf16[16,1024]{1,0:T(8,128)(2,1)S(1)} %copy-done), channel_id=1, source_target_pairs={{0,128},{8,136},{16,144},{24,152},{32,160},{40,168},{48,176},{56,1... | collective-permute-start | bytes 98312 | tf_op jit(solution)/shard_map/ppermute | solution.py:277
  26.7 5.4 %collective-permute-start.1 = (bf16[144,128]{1,0:T(8,128)(2,1)S(1)}, bf16[144,128]{1,0:T(8,128)(2,1)S(1)}, u32[]{:S(2)}, u32[]{:S(2)}) collective-permute-start(bf16[144,128]{1,0:T(8,128)(2,1)S(1)} %partner.1), channel_id=1, source_target_pairs={{0,128},{8,136},{16,144},{24,152},{32,160},{40,168},{48,176},{56,1... | collective-permute-start | bytes 110600 | tf_op jit(solution)/shard_map/ppermute | solution.py:311
  33.0 4.1 %collective-permute-start.3 = (bf16[16,1024]{1,0:T(8,128)(2,1)S(1)}, bf16[16,1024]{1,0:T(8,128)(2,1)S(1)}, u32[]{:S(2)}, u32[]{:S(2)}) collective-permute-start(bf16[16,1024]{1,0:T(8,128)(2,1)S(1)} %get-tuple-element.38), channel_id=1, source_target_pairs={{0,2},{1,3},{2,0},{3,1},{4,6},{5,7},{6,4},{7,5},{8,10},{9,11},{10,... | collective-permute-start | bytes 98312 | tf_op jit(solution)/shard_map/ppermute | solution.py:349
  35.8 4.0 %collective-permute-start.2 = (bf16[16,1024]{1,0:T(8,128)(2,1)S(1)}, bf16[16,1024]{1,0:T(8,128)(2,1)S(1)}, u32[]{:S(2)}, u32[]{:S(2)}) collective-permute-start(bf16[16,1024]{1,0:T(8,128)(2,1)S(1)} %get-tuple-element.37), channel_id=1, source_target_pairs={{0,2},{1,3},{2,0},{3,1},{4,6},{5,7},{6,4},{7,5},{8,10},{9,11},{10,... | collective-permute-start | bytes 98312 | tf_op jit(solution)/shard_map/ppermute | solution.py:349
  37.1 5.2 %collective-permute-start.4 = (bf16[16,1024]{1,0:T(8,128)(2,1)S(1)}, bf16[16,1024]{1,0:T(8,128)(2,1)S(1)}, u32[]{:S(2)}, u32[]{:S(2)}) collective-permute-start(bf16[16,1024]{1,0:T(8,128)(2,1)S(1)} %fusion), channel_id=1, source_target_pairs={{0,6},{1,7},{2,4},{3,5},{4,2},{5,3},{6,0},{7,1},{8,14},{9,15},{10,... | collective-permute-start | bytes 98312 | tf_op jit(solution)/shard_map/ppermute | solution.py:349
  42.4 7.9 %collective-permute-start.5 = (bf16[16,512]{1,0:T(8,128)(2,1)S(1)}, bf16[16,512]{1,0:T(8,128)(2,1)S(1)}, u32[]{:S(2)}, u32[]{:S(2)}) collective-permute-start(bf16[16,512]{1,0:T(8,128)(2,1)S(1)} %select_convert_fusion), channel_id=1, source_target_pairs={{0,1},{1,0},{2,3},{3,2},{4,5},{5,4},{6,7},{7,6},{8,9},{9,8},{10,11... | collective-permute-start | bytes 49160 | tf_op jit(solution)/shard_map/ppermute | solution.py:359

commit v8 on v6

--- a/solution.py
+++ b/solution.py
@@ -349,12 +349,13 @@
         return lax.ppermute(x, "tensor", [(2 * i + k, 2 * partner(i) + k) for i in range(pieces // 2) for k in range(2)])
 
     sums = keep.astype(jnp.float32) + trade(send, lambda i: i ^ 1).astype(jnp.float32)
-    sums = sums[0] + trade(sums[1].astype(jnp.bfloat16), lambda i: 3 - i).astype(jnp.float32)
-    halves = jnp.split(sums, 2, axis=1)
+    halves = jnp.split(sums, 2, axis=2)
     away = jnp.where(second, halves[0], halves[1]).astype(jnp.bfloat16)
     near = jnp.where(second, halves[1], halves[0])
     away = lax.ppermute(away, "tensor", [(i, i ^ 1) for i in range(pieces)])
-    return (near + away.astype(jnp.float32)).astype(jnp.bfloat16)
+    sums = near + away.astype(jnp.float32)
+    other = trade(sums[1].astype(jnp.bfloat16), lambda i: 3 - i)
+    return (sums[0] + other.astype(jnp.float32)).astype(jnp.bfloat16)
 
 
 def solution(mesh):

time: 51.2 us -> 51.2 us (level)
  no operation moved by 1% of the time
where the time goes in v8:
time: 51.2 us; the launch traced here: 50.9 us
  starting transfers between devices  19.7 us (38%)
  waiting for transfers between devices  19.4 us (38%)
  Pallas kernels  11.1 us (22%)
  other arithmetic  0.65 us (1%)
    ppermute x1, waiting for transfers between devices, shards(): far_queries = lax.ppermute(queries, 'pool', swap)  7.11 us
    ppermute x2, waiting for transfers between devices, trade(): lax.ppermute(x, 'tensor', [(2 * i + k, 2 * partner(i) + k) for i in range...  6.01 us
    ppermute x1, starting transfers between devices, shards(): away = lax.ppermute(away, 'tensor', [(i, i ^ 1) for i in range(pieces)])  5.99 us
    all_to_all x1, starting transfers between devices, shards(): got = lax.all_to_all(packed, 'pool', 0, 0, axis_index_groups=halves)  5.94 us
    all_to_all x1, waiting for transfers between devices, shards(): got = lax.all_to_all(packed, 'pool', 0, 0, axis_index_groups=halves)  4.28 us
    ppermute x1, starting transfers between devices, shards(): far_queries = lax.ppermute(queries, 'pool', swap)  3.36 us
    pallas_call x1, Pallas kernels, shards(): pl.pallas_call(functools.partial(cache_kernel, scale), out_shape=[jax.Sha...  3.24 us
    ppermute x1, starting transfers between devices, shards(): back = lax.ppermute(back, 'pool', swap)  3.05 us
  transfers between devices with their start and end apart: 6, of which 5 were waited for; matrix products, arithmetic and copies ran while one was open for 0% of the time, Pallas kernels for 15%

profile of v8, /device:TPU:6, one launch (start us, length us, event | category | flops | bytes accessed | tf_op | source)
XLA Modules:
  0.0 50.9 jit_solution(15713736283485794968)
XLA Ops:
  0.0 0.0 copy-start
  0.0 2.2 %pack.1 = bf16[16,272,128]{2,1,0:T(8,128)(2,1)} custom-call(s32[32]{0:T(128)} %bitcast.9, s32[32]{0:T(128)} %dest_hbm.1, s32[32]{0:T(128)} %len_hbm.1, bf16[32,32,128]{2,1,0:T(8,128)(2,1)} %keys_hbm.1, bf16[32,32,128]{2,1,0:T(8,128)(2,1)} %values_hbm.1), custom_call_target="tpu_custom_call" | custom-call | tf_op jit(solution)/shard_map/pack/pallas_call | solution.py:278
  2.2 5.9 %all-to-all-start = ((bf16[16,272,128]{2,1,0:T(8,128)(2,1)}), bf16[16,272,128]{2,1,0:T(8,128)(2,1)S(1)}, u32[]{:S(2)}, u32[]{:S(2)}) async-start(bf16[16,272,128]{2,1,0:T(8,128)(2,1)} %pack.1), calls=%async_computation | async-start | bytes 2228224 | tf_op jit(solution)/shard_map/all_to_all | solution.py:290
  8.2 0.0 copy-done
  8.2 3.4 %collective-permute-start = (bf16[16,1024]{1,0:T(8,128)(2,1)S(1)}, bf16[16,1024]{1,0:T(8,128)(2,1)S(1)}, u32[]{:S(2)}, u32[]{:S(2)}) collective-permute-start(bf16[16,1024]{1,0:T(8,128)(2,1)S(1)} %copy-done), channel_id=1, source_target_pairs={{0,128},{8,136},{16,144},{24,152},{32,160},{40,168},{48,176},{56,1... | collective-permute-start | bytes 98312 | tf_op jit(solution)/shard_map/ppermute | solution.py:277
  11.6 3.2 %cache.1 = (f32[128,128]{1,0:T(8,128)S(1)}, f32[128,128]{1,0:T(8,128)S(1)}, f32[128,128]{1,0:T(8,128)S(1)}, f32[128,128]{1,0:T(8,128)S(1)}, bf16[256,4096]{1,0:T(8,128)(2,1)S(1)}) custom-call(s32[16]{0:T(128)} %lens_ref.1, bf16[16,1024]{1,0:T(8,128)(2,1)} %q_ref.1, bf16[16,256,128]{2,1,0:T(8,128)(2,1)} %keys_ref.1, bf16[16,256,128]{2,1,0:T(8,128)(2,1)} %values_ref.1, ...), custom_call_target="tpu_custom_call" | custom-call | flops 200000000 | bytes 12000000 | tf_op jit(solution)/shard_map/cache/pallas_call | solution.py:291
  14.8 7.1 %collective-permute-done.q_ref = bf16[16,1024]{1,0:T(8,128)(2,1)S(1)} collective-permute-done((bf16[16,1024]{1,0:T(8,128)(2,1)S(1)}, bf16[16,1024]{1,0:T(8,128)(2,1)S(1)}, u32[]{:S(2)}, u32[]{:S(2)}) %collective-permute-start) | collective-permute-done | bytes 32800 | tf_op jit(solution)/shard_map/ppermute | solution.py:277
  21.9 4.3 %all-to-all-done.got_ref = bf16[16,272,128]{2,1,0:T(8,128)(2,1)S(1)} async-done(((bf16[16,272,128]{2,1,0:T(8,128)(2,1)}), bf16[16,272,128]{2,1,0:T(8,128)(2,1)S(1)}, u32[]{:S(2)}, u32[]{:S(2)}) %all-to-all-start) | async-done | bytes 1114144 | tf_op jit(solution)/shard_map/all_to_all | solution.py:290
  26.2 0.5 %partner.1 = bf16[144,128]{1,0:T(8,128)(2,1)S(1)} custom-call(bf16[16,1024]{1,0:T(8,128)(2,1)S(1)} %collective-permute-done.q_ref, bf16[16,272,128]{2,1,0:T(8,128)(2,1)S(1)} %all-to-all-done.got_ref), custom_call_target="tpu_custom_call" | custom-call | tf_op jit(solution)/shard_map/partner/pallas_call | solution.py:302
  26.7 3.1 %collective-permute-start.1 = (bf16[144,128]{1,0:T(8,128)(2,1)S(1)}, bf16[144,128]{1,0:T(8,128)(2,1)S(1)}, u32[]{:S(2)}, u32[]{:S(2)}) collective-permute-start(bf16[144,128]{1,0:T(8,128)(2,1)S(1)} %partner.1), channel_id=1, source_target_pairs={{0,128},{8,136},{16,144},{24,152},{32,160},{40,168},{48,176},{56,1... | collective-permute-start | bytes 110600 | tf_op jit(solution)/shard_map/ppermute | solution.py:311
  29.8 2.3 %own.1 = (f32[128,128]{1,0:T(8,128)S(1)}, f32[128,128]{1,0:T(8,128)S(1)}, f32[128,128]{1,0:T(8,128)S(1)}, bf16[256,4096]{1,0:T(8,128)(2,1)S(1)}, bf16[2,512,1024]{2,1,0:T(8,128)(2,1)S(1)}) custom-call(f32[128,128]{1,0:T(8,128)S(1)} %get-tuple-element.21.q_ref, bf16[16,272,128]{2,1,0:T(8,128)(2,1)S(1)} %all-to-all-done.got_ref, ...), custom_call_target="tpu_custom_call" | custom-call | flops 100000000 | bytes 2000000 | tf_op jit(solution)/shard_map/own/pallas_call | solution.py:313
  32.1 0.0 collective-permute-done.1.back_ref
  32.1 0.9 %send.1 = (bf16[16,1024]{1,0:T(8,128)(2,1)S(1)}, bf16[2,16,1024]{2,1,0:T(8,128)(2,1)S(1)}) custom-call(f32[128,128]{1,0:T(8,128)S(1)} %get-tuple-element.26.main_ref, f32[128,128]{1,0:T(8,128)S(1)} %get-tuple-element.27.top_ref, f32[128,128]{1,0:T(8,128)S(1)} %get-tuple-element.28.sum_ref, bf16[144,128]{1,0:T(8,128)(2,1)S(1)} %collective-permute-done.1.back_ref, ...), custom_call_target="tpu_custom_call" | custom-call | tf_op jit(solution)/shard_map/send/pallas_call | solution.py:326
  33.0 0.8 %collective-permute-start.2 = (bf16[2,16,1024]{2,1,0:T(8,128)(2,1)S(1)}, bf16[2,16,1024]{2,1,0:T(8,128)(2,1)S(1)}, u32[]{:S(2)}, u32[]{:S(2)}) collective-permute-start(bf16[2,16,1024]{2,1,0:T(8,128)(2,1)S(1)} %get-tuple-element.36), channel_id=1, source_target_pairs={{0,2},{1,3},{2,0},{3,1},{4,6},{5,7},{6,4},{7,5},{8,10},{9,11},{10,... | collective-permute-start | bytes 196616 | tf_op jit(solution)/shard_map/ppermute | solution.py:349
  33.8 1.9 %keep.1 = bf16[2,16,1024]{2,1,0:T(8,128)(2,1)S(1)} custom-call(bf16[16,1024]{1,0:T(8,128)(2,1)S(1)} %get-tuple-element.33.attended_ref, bf16[256,4096]{1,0:T(8,128)(2,1)S(1)} %get-tuple-element.30.weight0_ref, bf16[256,4096]{1,0:T(8,128)(2,1)S(1)} %get-tuple-element.31.weight1_ref, bf16[1024,4096]{1,0:T(8,128)(2,1)} %weight_hbm.5), custom_call_target="tpu_custom_call" | custom-call | flops 8000000000 | bytes 16000000 | tf_op jit(solution)/shard_map/keep/pallas_call | solution.py:335
  35.7 1.5 %collective-permute-done.2 = bf16[2,16,1024]{2,1,0:T(8,128)(2,1)S(1)} collective-permute-done((bf16[2,16,1024]{2,1,0:T(8,128)(2,1)S(1)}, bf16[2,16,1024]{2,1,0:T(8,128)(2,1)S(1)}, u32[]{:S(2)}, u32[]{:S(2)}) %collective-permute-start.2) | collective-permute-done | bytes 65568 | tf_op jit(solution)/shard_map/ppermute | solution.py:349
  37.3 6.0 %collective-permute-start.3 = (bf16[2,16,512]{2,1,0:T(8,128)(2,1)S(1)}, bf16[2,16,512]{2,1,0:T(8,128)(2,1)S(1)}, u32[]{:S(2)}, u32[]{:S(2)}) collective-permute-start(bf16[2,16,512]{2,1,0:T(8,128)(2,1)S(1)} %select_convert_fusion), channel_id=1, source_target_pairs={{0,1},{1,0},{2,3},{3,2},{4,5},{5,4},{6,7},{7,6},{8,9},{9,8},{10,11... | collective-permute-start | bytes 98312 | tf_op jit(solution)/shard_map/ppermute | solution.py:355
  43.3 1.9 %collective-permute-done.3 = bf16[2,16,512]{2,1,0:T(8,128)(2,1)S(1)} collective-permute-done((bf16[2,16,512]{2,1,0:T(8,128)(2,1)S(1)}, bf16[2,16,512]{2,1,0:T(8,128)(2,1)S(1)}, u32[]{:S(2)}, u32[]{:S(2)}) %collective-permute-start.3) | collective-permute-done | bytes 32800 | tf_op jit(solution)/shard_map/ppermute | solution.py:355
  45.3 0.6 %collective-permute-start.4 = (bf16[16,512]{1,0:T(8,128)(2,1)S(1)}, bf16[16,512]{1,0:T(8,128)(2,1)S(1)}, u32[]{:S(2)}, u32[]{:S(2)}) collective-permute-start(bf16[16,512]{1,0:T(8,128)(2,1)S(1)} %fusion.2), channel_id=1, source_target_pairs={{0,6},{1,7},{2,4},{3,5},{4,2},{5,3},{6,0},{7,1},{8,14},{9,15},{10,... | collective-permute-start | bytes 49160 | tf_op jit(solution)/shard_map/ppermute | solution.py:349
  45.8 4.5 %collective-permute-done.4 = bf16[16,512]{1,0:T(8,128)(2,1)S(1)} collective-permute-done((bf16[16,512]{1,0:T(8,128)(2,1)S(1)}, bf16[16,512]{1,0:T(8,128)(2,1)S(1)}, u32[]{:S(2)}, u32[]{:S(2)}) %collective-permute-start.4) | collective-permute-done | bytes 16416 | tf_op jit(solution)/shard_map/ppermute | solution.py:349
  50.3 0.6 %fusion.1 = bf16[16,512]{1,0:T(8,128)(2,1)} fusion(f32[2,16,512]{2,1,0:T(8,128)S(1)} %convert_add_fusion.1, bf16[16,512]{1,0:T(8,128)(2,1)S(1)} %collective-permute-done.4), kind=kLoop, calls=%fused_computation.6 | loop fusion | flops 24576 | bytes 65536 | tf_op jit(solution)/shard_map/convert_element_type | solution.py:358
  (4 shorter events, 0.0 us)
Async XLA Ops:
  0.0 8.2 %copy-start = (bf16[16,1024]{1,0:T(8,128)(2,1)S(1)}, bf16[16,1024]{1,0:T(8,128)(2,1)}, u32[]{:S(2)}) copy-start(bf16[16,1024]{1,0:T(8,128)(2,1)} %q_ref.1) | copy-start | bytes 98308
  2.2 24.0 %all-to-all-start = ((bf16[16,272,128]{2,1,0:T(8,128)(2,1)}), bf16[16,272,128]{2,1,0:T(8,128)(2,1)S(1)}, u32[]{:S(2)}, u32[]{:S(2)}) async-start(bf16[16,272,128]{2,1,0:T(8,128)(2,1)} %pack.1), calls=%async_computation | async-start | bytes 2228224 | tf_op jit(solution)/shard_map/all_to_all | solution.py:290
  8.2 13.7 %collective-permute-start = (bf16[16,1024]{1,0:T(8,128)(2,1)S(1)}, bf16[16,1024]{1,0:T(8,128)(2,1)S(1)}, u32[]{:S(2)}, u32[]{:S(2)}) collective-permute-start(bf16[16,1024]{1,0:T(8,128)(2,1)S(1)} %copy-done), channel_id=1, source_target_pairs={{0,128},{8,136},{16,144},{24,152},{32,160},{40,168},{48,176},{56,1... | collective-permute-start | bytes 98312 | tf_op jit(solution)/shard_map/ppermute | solution.py:277
  26.7 5.4 %collective-permute-start.1 = (bf16[144,128]{1,0:T(8,128)(2,1)S(1)}, bf16[144,128]{1,0:T(8,128)(2,1)S(1)}, u32[]{:S(2)}, u32[]{:S(2)}) collective-permute-start(bf16[144,128]{1,0:T(8,128)(2,1)S(1)} %partner.1), channel_id=1, source_target_pairs={{0,128},{8,136},{16,144},{24,152},{32,160},{40,168},{48,176},{56,1... | collective-permute-start | bytes 110600 | tf_op jit(solution)/shard_map/ppermute | solution.py:311
  33.0 4.3 %collective-permute-start.2 = (bf16[2,16,1024]{2,1,0:T(8,128)(2,1)S(1)}, bf16[2,16,1024]{2,1,0:T(8,128)(2,1)S(1)}, u32[]{:S(2)}, u32[]{:S(2)}) collective-permute-start(bf16[2,16,1024]{2,1,0:T(8,128)(2,1)S(1)} %get-tuple-element.36), channel_id=1, source_target_pairs={{0,2},{1,3},{2,0},{3,1},{4,6},{5,7},{6,4},{7,5},{8,10},{9,11},{10,... | collective-permute-start | bytes 196616 | tf_op jit(solution)/shard_map/ppermute | solution.py:349
  37.3 7.9 %collective-permute-start.3 = (bf16[2,16,512]{2,1,0:T(8,128)(2,1)S(1)}, bf16[2,16,512]{2,1,0:T(8,128)(2,1)S(1)}, u32[]{:S(2)}, u32[]{:S(2)}) collective-permute-start(bf16[2,16,512]{2,1,0:T(8,128)(2,1)S(1)} %select_convert_fusion), channel_id=1, source_target_pairs={{0,1},{1,0},{2,3},{3,2},{4,5},{5,4},{6,7},{7,6},{8,9},{9,8},{10,11... | collective-permute-start | bytes 98312 | tf_op jit(solution)/shard_map/ppermute | solution.py:355
  45.3 5.0 %collective-permute-start.4 = (bf16[16,512]{1,0:T(8,128)(2,1)S(1)}, bf16[16,512]{1,0:T(8,128)(2,1)S(1)}, u32[]{:S(2)}, u32[]{:S(2)}) collective-permute-start(bf16[16,512]{1,0:T(8,128)(2,1)S(1)} %fusion.2), channel_id=1, source_target_pairs={{0,6},{1,7},{2,4},{3,5},{4,2},{5,3},{6,0},{7,1},{8,14},{9,15},{10,... | collective-permute-start | bytes 49160 | tf_op jit(solution)/shard_map/ppermute | solution.py:349
